TPU v7x, 32 devices: a whole 2x2x4 slice. The times are simulated.
32 devices in a mesh: row: 16 (over z, x, core), col: 2 (over y).
Axes of the slice: x: 2, y: 2, z: 4, core: 2. Of those that a mesh axis runs over, the one named last changes fastest.
Arguments:
- eig_slab: float32 [8192, 4096], P('row', 'col'), may hold values from -6 to 6
- reflectors: float32 [16, 8192], P('col', 'row'), may hold values from -6 to 6
- row_offsets: int32 [16], replicated, may hold values from 1 to 24, as said below
Outputs:
- rotated: float32 [8192, 4096], P('row', 'col')
Inputs may be any that keep to these rules, and one draw needn't show every extreme that they name: row_offsets[0] is 1; each next one is 1 or 2 larger than the one before, and exactly 8 of these steps are 2.
All inputs are finite; a program needn't handle non-finite values.
Results may differ from a plain program's by a relative error of at most 0.00027.
Values sent between devices are 32-bit elements; how exact they have to be, the bound alone decides.
No kernel may reach another device: no remote copies, remote signals or barrier semaphores. Data moves between devices by JAX's collectives and lax.ppermute only.
A program may use at most 64 MiB of HBM per device.

v0:
```python
import jax
import jax.numpy as jnp
from jax import lax
from jax.sharding import PartitionSpec as P

WIDTH = 64
SWEEPS = 16


def extended_2(cells, sides, width):
    for axis, dim in sides:
        count = lax.axis_size(axis)
        ends = count - 1
        head = lax.slice_in_dim(cells, 0, width, axis=dim)
        tail = lax.slice_in_dim(cells, cells.shape[dim] - width, cells.shape[dim], axis=dim)
        cells = jnp.concatenate(
            [
                lax.ppermute(tail, axis, [(i, (i + 1) % count) for i in range(ends)]),
                cells,
                lax.ppermute(head, axis, [((i + 1) % count, i) for i in range(ends)]),
            ],
            axis=dim,
        )
    return cells


def apply_sweep(eig_rows, eigen_columns, first_row, row_displacement, row_count_total, band_width):
    length, columns = eig_rows.shape
    overall_row_span = first_row + jnp.arange(length, dtype=jnp.int32)
    active_flags = (overall_row_span >= row_displacement) & (overall_row_span < row_count_total)
    eigen_columns = jnp.where(active_flags, eigen_columns, jnp.float32(0.0))
    shift = jnp.mod(row_displacement - first_row, band_width)
    zero_rows = jnp.zeros((band_width, columns), eig_rows.dtype)
    padded = jnp.concatenate([zero_rows, eig_rows, zero_rows], axis=0)
    zero_vec = jnp.zeros((band_width,), eigen_columns.dtype)
    padded_vec = jnp.concatenate([zero_vec, eigen_columns, zero_vec])
    integer_nought = jnp.zeros((band_width,), jnp.int32)
    extended_active_flags = jnp.concatenate(
        [integer_nought, active_flags.astype(jnp.int32), integer_nought]
    )
    windows_count = (length + band_width) // band_width
    windows = lax.dynamic_slice_in_dim(padded, shift, length + band_width, 0).reshape(
        windows_count, band_width, columns
    )
    window_vecs = lax.dynamic_slice_in_dim(padded_vec, shift, length + band_width, 0).reshape(
        windows_count, band_width
    )
    live_count = jnp.sum(
        lax.dynamic_slice_in_dim(extended_active_flags, shift, length + band_width, 0).reshape(
            windows_count, band_width
        ),
        axis=1,
    )
    squares = jnp.sum(window_vecs * window_vecs, axis=1)
    factor = jnp.where(
        live_count > 0, 2.0 / (squares + (live_count == 0).astype(jnp.float32)), jnp.float32(0.0)
    )
    project = jnp.einsum("wr,wrc->wc", window_vecs, windows, precision=lax.Precision.HIGHEST)
    updated = windows - (factor[:, None] * window_vecs)[:, :, None] * project[:, None, :]
    padded = lax.dynamic_update_slice_in_dim(
        padded, updated.reshape(length + band_width, columns), shift, 0
    )
    return padded[band_width : band_width + length]


def local(eig_slab, reflectors, row_offsets):
    local_rows = eig_slab.shape[0]
    row_count_total = local_rows * lax.axis_size("row")
    depth = 1
    margin = depth * WIDTH
    base_row = lax.axis_index("row") * local_rows
    first_row = base_row - margin
    vec_rims = extended_2(reflectors, (("row", 1),), margin)
    all_vectors = lax.all_gather(vec_rims, "col", axis=0, tiled=True)

    def one_round(round_index, current):
        extended = extended_2(current, (("row", 0),), margin)
        sweep_index = round_index * depth + 0
        eigen_columns = lax.dynamic_index_in_dim(all_vectors, sweep_index, 0, keepdims=False)
        row_displacement = lax.dynamic_index_in_dim(row_offsets, sweep_index, 0, keepdims=False)
        extended = apply_sweep(
            extended, eigen_columns, first_row, row_displacement, row_count_total, WIDTH
        )
        return extended[margin : margin + local_rows]

    return lax.fori_loop(0, SWEEPS // depth, one_round, eig_slab)


def solution(mesh):
    placed = (P("row", "col"), P("col", "row"), P())
    return jax.shard_map(
        local, mesh=mesh, in_specs=placed, out_specs=P("row", "col"), check_vma=False
    )
```

profile of v0, /device:TPU:10, one launch (start us, length us, event | category | flops | bytes accessed | tf_op | source)
XLA Modules:
  0.0 747.6 jit_solution(16013258136215270068)
XLA Ops:
  0.0 4.7 copy.22
  11.8 4.4 all_gather.3
  16.2 731.4 %while.15 = (s32[]{:T(128)}, f32[512,2048]{1,0:T(8,128)}, s32[16]{0:T(128)S(1)}, s32[]{:T(128)}, f32[16,640]{1,0:T(8,128)S(1)}, /*index=5*/s32[]{:T(128)}, f32[]...) while((s32[]{:T(128)}, f32[512,2048]{1,0:T(8,128)}, s32[16]{0:T(128)S(1)}, s32[]{:T(128)}, ...), condition=%wide.region_3.4_spmd, body=%wide.region_0.3_spmd.sunk | while | flops 20197436 | bytes 92192944 | solution.py:86
  41.0 15.6 %dynamic_update_slice.11 = f32[768,2048]{1,0:T(8,128)} dynamic-update-slice(f32[768,2048]{1,0:T(8,128)} %copy-done, f32[704,2048]{1,0:T(8,128)} %fusion.22, s32[]{:T(128)S(6)} %select_n.79, s32[]{:T(128)} %constant.107.clone.1..sunk) | dynamic-update-slice | bytes 11534340 | tf_op jit(solution)/shard_map/while/body/eval_jaxpr/dynamic_update_slice | solution.py:60
  56.6 4.7 slice.52
  64.5 3.8 collective-permute-start.1
  72.0 6.9 collective-permute-done
  88.9 15.6 %dynamic_update_slice.11 = f32[768,2048]{1,0:T(8,128)} dynamic-update-slice(f32[768,2048]{1,0:T(8,128)} %copy-done, f32[704,2048]{1,0:T(8,128)} %fusion.22, s32[]{:T(128)S(6)} %select_n.79, s32[]{:T(128)} %constant.107.clone.1..sunk) | dynamic-update-slice | bytes 11534340 | tf_op jit(solution)/shard_map/while/body/eval_jaxpr/dynamic_update_slice | solution.py:60
  104.6 4.7 slice.52
  119.8 6.9 collective-permute-done
  136.7 15.6 %dynamic_update_slice.11 = f32[768,2048]{1,0:T(8,128)} dynamic-update-slice(f32[768,2048]{1,0:T(8,128)} %copy-done, f32[704,2048]{1,0:T(8,128)} %fusion.22, s32[]{:T(128)S(6)} %select_n.79, s32[]{:T(128)} %constant.107.clone.1..sunk) | dynamic-update-slice | bytes 11534340 | tf_op jit(solution)/shard_map/while/body/eval_jaxpr/dynamic_update_slice | solution.py:60
  152.3 4.7 slice.52
  160.2 3.6 collective-permute-start.1
  167.5 6.9 collective-permute-done
  184.5 15.6 %dynamic_update_slice.11 = f32[768,2048]{1,0:T(8,128)} dynamic-update-slice(f32[768,2048]{1,0:T(8,128)} %copy-done, f32[704,2048]{1,0:T(8,128)} %fusion.22, s32[]{:T(128)S(6)} %select_n.79, s32[]{:T(128)} %constant.107.clone.1..sunk) | dynamic-update-slice | bytes 11534340 | tf_op jit(solution)/shard_map/while/body/eval_jaxpr/dynamic_update_slice | solution.py:60
  200.1 4.7 slice.52
  228.6 15.6 %dynamic_update_slice.11 = f32[768,2048]{1,0:T(8,128)} dynamic-update-slice(f32[768,2048]{1,0:T(8,128)} %copy-done, f32[704,2048]{1,0:T(8,128)} %fusion.22, s32[]{:T(128)S(6)} %select_n.79, s32[]{:T(128)} %constant.107.clone.1..sunk) | dynamic-update-slice | bytes 11534340 | tf_op jit(solution)/shard_map/while/body/eval_jaxpr/dynamic_update_slice | solution.py:60
  244.3 4.7 slice.52
  259.5 5.5 collective-permute-done
  275.1 15.6 %dynamic_update_slice.11 = f32[768,2048]{1,0:T(8,128)} dynamic-update-slice(f32[768,2048]{1,0:T(8,128)} %copy-done, f32[704,2048]{1,0:T(8,128)} %fusion.22, s32[]{:T(128)S(6)} %select_n.79, s32[]{:T(128)} %constant.107.clone.1..sunk) | dynamic-update-slice | bytes 11534340 | tf_op jit(solution)/shard_map/while/body/eval_jaxpr/dynamic_update_slice | solution.py:60
  290.7 4.7 slice.52
  298.6 3.6 collective-permute-start.1
  319.1 15.6 %dynamic_update_slice.11 = f32[768,2048]{1,0:T(8,128)} dynamic-update-slice(f32[768,2048]{1,0:T(8,128)} %copy-done, f32[704,2048]{1,0:T(8,128)} %fusion.22, s32[]{:T(128)S(6)} %select_n.79, s32[]{:T(128)} %constant.107.clone.1..sunk) | dynamic-update-slice | bytes 11534340 | tf_op jit(solution)/shard_map/while/body/eval_jaxpr/dynamic_update_slice | solution.py:60
  334.7 4.7 slice.52
  342.6 3.6 collective-permute-start.1
  349.9 5.5 collective-permute-done
  365.5 15.6 %dynamic_update_slice.11 = f32[768,2048]{1,0:T(8,128)} dynamic-update-slice(f32[768,2048]{1,0:T(8,128)} %copy-done, f32[704,2048]{1,0:T(8,128)} %fusion.22, s32[]{:T(128)S(6)} %select_n.79, s32[]{:T(128)} %constant.107.clone.1..sunk) | dynamic-update-slice | bytes 11534340 | tf_op jit(solution)/shard_map/while/body/eval_jaxpr/dynamic_update_slice | solution.py:60
  381.2 4.7 slice.52
  409.5 15.6 %dynamic_update_slice.11 = f32[768,2048]{1,0:T(8,128)} dynamic-update-slice(f32[768,2048]{1,0:T(8,128)} %copy-done, f32[704,2048]{1,0:T(8,128)} %fusion.22, s32[]{:T(128)S(6)} %select_n.79, s32[]{:T(128)} %constant.107.clone.1..sunk) | dynamic-update-slice | bytes 11534340 | tf_op jit(solution)/shard_map/while/body/eval_jaxpr/dynamic_update_slice | solution.py:60
  425.2 4.7 slice.52
  440.4 5.5 collective-permute-done
  456.0 15.6 %dynamic_update_slice.11 = f32[768,2048]{1,0:T(8,128)} dynamic-update-slice(f32[768,2048]{1,0:T(8,128)} %copy-done, f32[704,2048]{1,0:T(8,128)} %fusion.22, s32[]{:T(128)S(6)} %select_n.79, s32[]{:T(128)} %constant.107.clone.1..sunk) | dynamic-update-slice | bytes 11534340 | tf_op jit(solution)/shard_map/while/body/eval_jaxpr/dynamic_update_slice | solution.py:60
  471.6 4.7 slice.52
  500.0 15.6 %dynamic_update_slice.11 = f32[768,2048]{1,0:T(8,128)} dynamic-update-slice(f32[768,2048]{1,0:T(8,128)} %copy-done, f32[704,2048]{1,0:T(8,128)} %fusion.22, s32[]{:T(128)S(6)} %select_n.79, s32[]{:T(128)} %constant.107.clone.1..sunk) | dynamic-update-slice | bytes 11534340 | tf_op jit(solution)/shard_map/while/body/eval_jaxpr/dynamic_update_slice | solution.py:60
  515.6 4.7 slice.52
  530.8 5.5 collective-permute-done
  546.4 15.6 %dynamic_update_slice.11 = f32[768,2048]{1,0:T(8,128)} dynamic-update-slice(f32[768,2048]{1,0:T(8,128)} %copy-done, f32[704,2048]{1,0:T(8,128)} %fusion.22, s32[]{:T(128)S(6)} %select_n.79, s32[]{:T(128)} %constant.107.clone.1..sunk) | dynamic-update-slice | bytes 11534340 | tf_op jit(solution)/shard_map/while/body/eval_jaxpr/dynamic_update_slice | solution.py:60
  562.0 4.7 slice.52
  590.4 15.6 %dynamic_update_slice.11 = f32[768,2048]{1,0:T(8,128)} dynamic-update-slice(f32[768,2048]{1,0:T(8,128)} %copy-done, f32[704,2048]{1,0:T(8,128)} %fusion.22, s32[]{:T(128)S(6)} %select_n.79, s32[]{:T(128)} %constant.107.clone.1..sunk) | dynamic-update-slice | bytes 11534340 | tf_op jit(solution)/shard_map/while/body/eval_jaxpr/dynamic_update_slice | solution.py:60
  606.0 4.7 slice.52
  621.3 5.5 collective-permute-done
  636.8 15.6 %dynamic_update_slice.11 = f32[768,2048]{1,0:T(8,128)} dynamic-update-slice(f32[768,2048]{1,0:T(8,128)} %copy-done, f32[704,2048]{1,0:T(8,128)} %fusion.22, s32[]{:T(128)S(6)} %select_n.79, s32[]{:T(128)} %constant.107.clone.1..sunk) | dynamic-update-slice | bytes 11534340 | tf_op jit(solution)/shard_map/while/body/eval_jaxpr/dynamic_update_slice | solution.py:60
  652.5 4.7 slice.52
  680.8 15.6 %dynamic_update_slice.11 = f32[768,2048]{1,0:T(8,128)} dynamic-update-slice(f32[768,2048]{1,0:T(8,128)} %copy-done, f32[704,2048]{1,0:T(8,128)} %fusion.22, s32[]{:T(128)S(6)} %select_n.79, s32[]{:T(128)} %constant.107.clone.1..sunk) | dynamic-update-slice | bytes 11534340 | tf_op jit(solution)/shard_map/while/body/eval_jaxpr/dynamic_update_slice | solution.py:60
  696.5 4.7 slice.52
  711.7 5.5 collective-permute-done
  727.3 15.6 %dynamic_update_slice.11 = f32[768,2048]{1,0:T(8,128)} dynamic-update-slice(f32[768,2048]{1,0:T(8,128)} %copy-done, f32[704,2048]{1,0:T(8,128)} %fusion.22, s32[]{:T(128)S(6)} %select_n.79, s32[]{:T(128)} %constant.107.clone.1..sunk) | dynamic-update-slice | bytes 11534340 | tf_op jit(solution)/shard_map/while/body/eval_jaxpr/dynamic_update_slice | solution.py:60
  742.9 4.7 slice.52
  (557 shorter events, 331.5 us)
Async XLA Ops:
  0.0 4.7 copy-start.1
  0.0 16.2 %copy-start.2 = (s32[16]{0:T(128)S(1)}, s32[16]{0:T(128)}, u32[]{:S(2)}) copy-start(s32[16]{0:T(128)} %param.7) | copy-start | bytes 196
  4.8 5.6 collective-permute-start.2
  6.7 5.0 collective-permute-start.3
  17.5 10.5 %collective-permute-start = (f32[64,2048]{1,0:T(8,128)S(1)}, f32[64,2048]{1,0:T(8,128)S(1)}, u32[]{:S(2)}, u32[]{:S(2)}) collective-permute-start(f32[64,2048]{1,0:T(8,128)S(1)} %get-tuple-element.186), channel_id=1, source_target_pairs={{0,2},{2,4},{4,6},{6,8},{8,10},{10,12},{12,14},{14,16},{16,18},{18... | collective-permute-start | bytes 1572872 | tf_op jit(solution)/shard_map/while/body/eval_jaxpr/ppermute | solution.py:18
  20.8 12.7 %collective-permute-start.1 = (f32[64,2048]{1,0:T(8,128)S(1)}, f32[64,2048]{1,0:T(8,128)S(1)}, u32[]{:S(2)}, u32[]{:S(2)}) collective-permute-start(f32[64,2048]{1,0:T(8,128)S(1)} %get-tuple-element.187), channel_id=1, source_target_pairs={{2,0},{4,2},{6,4},{8,6},{10,8},{12,10},{14,12},{16,14},{18,16},{20... | collective-permute-start | bytes 1572872 | tf_op jit(solution)/shard_map/while/body/eval_jaxpr/ppermute | solution.py:20
  33.5 4.0 copy-start
  62.6 16.3 %collective-permute-start = (f32[64,2048]{1,0:T(8,128)S(1)}, f32[64,2048]{1,0:T(8,128)S(1)}, u32[]{:S(2)}, u32[]{:S(2)}) collective-permute-start(f32[64,2048]{1,0:T(8,128)S(1)} %get-tuple-element.186), channel_id=1, source_target_pairs={{0,2},{2,4},{4,6},{6,8},{8,10},{10,12},{12,14},{14,16},{16,18},{18... | collective-permute-start | bytes 1572872 | tf_op jit(solution)/shard_map/while/body/eval_jaxpr/ppermute | solution.py:18
  64.5 16.9 %collective-permute-start.1 = (f32[64,2048]{1,0:T(8,128)S(1)}, f32[64,2048]{1,0:T(8,128)S(1)}, u32[]{:S(2)}, u32[]{:S(2)}) collective-permute-start(f32[64,2048]{1,0:T(8,128)S(1)} %get-tuple-element.187), channel_id=1, source_target_pairs={{2,0},{4,2},{6,4},{8,6},{10,8},{12,10},{14,12},{16,14},{18,16},{20... | collective-permute-start | bytes 1572872 | tf_op jit(solution)/shard_map/while/body/eval_jaxpr/ppermute | solution.py:20
  81.5 4.0 copy-start
  110.5 16.1 %collective-permute-start = (f32[64,2048]{1,0:T(8,128)S(1)}, f32[64,2048]{1,0:T(8,128)S(1)}, u32[]{:S(2)}, u32[]{:S(2)}) collective-permute-start(f32[64,2048]{1,0:T(8,128)S(1)} %get-tuple-element.186), channel_id=1, source_target_pairs={{0,2},{2,4},{4,6},{6,8},{8,10},{10,12},{12,14},{14,16},{16,18},{18... | collective-permute-start | bytes 1572872 | tf_op jit(solution)/shard_map/while/body/eval_jaxpr/ppermute | solution.py:18
  112.5 16.7 %collective-permute-start.1 = (f32[64,2048]{1,0:T(8,128)S(1)}, f32[64,2048]{1,0:T(8,128)S(1)}, u32[]{:S(2)}, u32[]{:S(2)}) collective-permute-start(f32[64,2048]{1,0:T(8,128)S(1)} %get-tuple-element.187), channel_id=1, source_target_pairs={{2,0},{4,2},{6,4},{8,6},{10,8},{12,10},{14,12},{16,14},{18,16},{20... | collective-permute-start | bytes 1572872 | tf_op jit(solution)/shard_map/while/body/eval_jaxpr/ppermute | solution.py:20
  129.3 4.0 copy-start
  158.3 16.1 %collective-permute-start = (f32[64,2048]{1,0:T(8,128)S(1)}, f32[64,2048]{1,0:T(8,128)S(1)}, u32[]{:S(2)}, u32[]{:S(2)}) collective-permute-start(f32[64,2048]{1,0:T(8,128)S(1)} %get-tuple-element.186), channel_id=1, source_target_pairs={{0,2},{2,4},{4,6},{6,8},{8,10},{10,12},{12,14},{14,16},{16,18},{18... | collective-permute-start | bytes 1572872 | tf_op jit(solution)/shard_map/while/body/eval_jaxpr/ppermute | solution.py:18
  160.2 16.7 %collective-permute-start.1 = (f32[64,2048]{1,0:T(8,128)S(1)}, f32[64,2048]{1,0:T(8,128)S(1)}, u32[]{:S(2)}, u32[]{:S(2)}) collective-permute-start(f32[64,2048]{1,0:T(8,128)S(1)} %get-tuple-element.187), channel_id=1, source_target_pairs={{2,0},{4,2},{6,4},{8,6},{10,8},{12,10},{14,12},{16,14},{18,16},{20... | collective-permute-start | bytes 1572872 | tf_op jit(solution)/shard_map/while/body/eval_jaxpr/ppermute | solution.py:20
  177.0 4.0 copy-start
  206.1 12.5 %collective-permute-start = (f32[64,2048]{1,0:T(8,128)S(1)}, f32[64,2048]{1,0:T(8,128)S(1)}, u32[]{:S(2)}, u32[]{:S(2)}) collective-permute-start(f32[64,2048]{1,0:T(8,128)S(1)} %get-tuple-element.186), channel_id=1, source_target_pairs={{0,2},{2,4},{4,6},{6,8},{8,10},{10,12},{12,14},{14,16},{16,18},{18... | collective-permute-start | bytes 1572872 | tf_op jit(solution)/shard_map/while/body/eval_jaxpr/ppermute | solution.py:18
  208.0 13.1 %collective-permute-start.1 = (f32[64,2048]{1,0:T(8,128)S(1)}, f32[64,2048]{1,0:T(8,128)S(1)}, u32[]{:S(2)}, u32[]{:S(2)}) collective-permute-start(f32[64,2048]{1,0:T(8,128)S(1)} %get-tuple-element.187), channel_id=1, source_target_pairs={{2,0},{4,2},{6,4},{8,6},{10,8},{12,10},{14,12},{16,14},{18,16},{20... | collective-permute-start | bytes 1572872 | tf_op jit(solution)/shard_map/while/body/eval_jaxpr/ppermute | solution.py:20
  221.2 4.0 copy-start
  250.3 14.8 %collective-permute-start = (f32[64,2048]{1,0:T(8,128)S(1)}, f32[64,2048]{1,0:T(8,128)S(1)}, u32[]{:S(2)}, u32[]{:S(2)}) collective-permute-start(f32[64,2048]{1,0:T(8,128)S(1)} %get-tuple-element.186), channel_id=1, source_target_pairs={{0,2},{2,4},{4,6},{6,8},{8,10},{10,12},{12,14},{14,16},{16,18},{18... | collective-permute-start | bytes 1572872 | tf_op jit(solution)/shard_map/while/body/eval_jaxpr/ppermute | solution.py:18
  252.2 15.4 %collective-permute-start.1 = (f32[64,2048]{1,0:T(8,128)S(1)}, f32[64,2048]{1,0:T(8,128)S(1)}, u32[]{:S(2)}, u32[]{:S(2)}) collective-permute-start(f32[64,2048]{1,0:T(8,128)S(1)} %get-tuple-element.187), channel_id=1, source_target_pairs={{2,0},{4,2},{6,4},{8,6},{10,8},{12,10},{14,12},{16,14},{18,16},{20... | collective-permute-start | bytes 1572872 | tf_op jit(solution)/shard_map/while/body/eval_jaxpr/ppermute | solution.py:20
  267.7 4.0 copy-start
  296.7 12.4 %collective-permute-start = (f32[64,2048]{1,0:T(8,128)S(1)}, f32[64,2048]{1,0:T(8,128)S(1)}, u32[]{:S(2)}, u32[]{:S(2)}) collective-permute-start(f32[64,2048]{1,0:T(8,128)S(1)} %get-tuple-element.186), channel_id=1, source_target_pairs={{0,2},{2,4},{4,6},{6,8},{8,10},{10,12},{12,14},{14,16},{16,18},{18... | collective-permute-start | bytes 1572872 | tf_op jit(solution)/shard_map/while/body/eval_jaxpr/ppermute | solution.py:18
  298.6 13.0 %collective-permute-start.1 = (f32[64,2048]{1,0:T(8,128)S(1)}, f32[64,2048]{1,0:T(8,128)S(1)}, u32[]{:S(2)}, u32[]{:S(2)}) collective-permute-start(f32[64,2048]{1,0:T(8,128)S(1)} %get-tuple-element.187), channel_id=1, source_target_pairs={{2,0},{4,2},{6,4},{8,6},{10,8},{12,10},{14,12},{16,14},{18,16},{20... | collective-permute-start | bytes 1572872 | tf_op jit(solution)/shard_map/while/body/eval_jaxpr/ppermute | solution.py:20
  340.7 14.8 %collective-permute-start = (f32[64,2048]{1,0:T(8,128)S(1)}, f32[64,2048]{1,0:T(8,128)S(1)}, u32[]{:S(2)}, u32[]{:S(2)}) collective-permute-start(f32[64,2048]{1,0:T(8,128)S(1)} %get-tuple-element.186), channel_id=1, source_target_pairs={{0,2},{2,4},{4,6},{6,8},{8,10},{10,12},{12,14},{14,16},{16,18},{18... | collective-permute-start | bytes 1572872 | tf_op jit(solution)/shard_map/while/body/eval_jaxpr/ppermute | solution.py:18
  342.6 15.4 %collective-permute-start.1 = (f32[64,2048]{1,0:T(8,128)S(1)}, f32[64,2048]{1,0:T(8,128)S(1)}, u32[]{:S(2)}, u32[]{:S(2)}) collective-permute-start(f32[64,2048]{1,0:T(8,128)S(1)} %get-tuple-element.187), channel_id=1, source_target_pairs={{2,0},{4,2},{6,4},{8,6},{10,8},{12,10},{14,12},{16,14},{18,16},{20... | collective-permute-start | bytes 1572872 | tf_op jit(solution)/shard_map/while/body/eval_jaxpr/ppermute | solution.py:20
  358.1 4.0 copy-start
  387.1 12.4 %collective-permute-start = (f32[64,2048]{1,0:T(8,128)S(1)}, f32[64,2048]{1,0:T(8,128)S(1)}, u32[]{:S(2)}, u32[]{:S(2)}) collective-permute-start(f32[64,2048]{1,0:T(8,128)S(1)} %get-tuple-element.186), channel_id=1, source_target_pairs={{0,2},{2,4},{4,6},{6,8},{8,10},{10,12},{12,14},{14,16},{16,18},{18... | collective-permute-start | bytes 1572872 | tf_op jit(solution)/shard_map/while/body/eval_jaxpr/ppermute | solution.py:18
  389.1 13.0 %collective-permute-start.1 = (f32[64,2048]{1,0:T(8,128)S(1)}, f32[64,2048]{1,0:T(8,128)S(1)}, u32[]{:S(2)}, u32[]{:S(2)}) collective-permute-start(f32[64,2048]{1,0:T(8,128)S(1)} %get-tuple-element.187), channel_id=1, source_target_pairs={{2,0},{4,2},{6,4},{8,6},{10,8},{12,10},{14,12},{16,14},{18,16},{20... | collective-permute-start | bytes 1572872 | tf_op jit(solution)/shard_map/while/body/eval_jaxpr/ppermute | solution.py:20
  402.1 4.0 copy-start
  431.1 14.8 %collective-permute-start = (f32[64,2048]{1,0:T(8,128)S(1)}, f32[64,2048]{1,0:T(8,128)S(1)}, u32[]{:S(2)}, u32[]{:S(2)}) collective-permute-start(f32[64,2048]{1,0:T(8,128)S(1)} %get-tuple-element.186), channel_id=1, source_target_pairs={{0,2},{2,4},{4,6},{6,8},{8,10},{10,12},{12,14},{14,16},{16,18},{18... | collective-permute-start | bytes 1572872 | tf_op jit(solution)/shard_map/while/body/eval_jaxpr/ppermute | solution.py:18
  433.1 15.4 %collective-permute-start.1 = (f32[64,2048]{1,0:T(8,128)S(1)}, f32[64,2048]{1,0:T(8,128)S(1)}, u32[]{:S(2)}, u32[]{:S(2)}) collective-permute-start(f32[64,2048]{1,0:T(8,128)S(1)} %get-tuple-element.187), channel_id=1, source_target_pairs={{2,0},{4,2},{6,4},{8,6},{10,8},{12,10},{14,12},{16,14},{18,16},{20... | collective-permute-start | bytes 1572872 | tf_op jit(solution)/shard_map/while/body/eval_jaxpr/ppermute | solution.py:20
  448.5 4.0 copy-start
  477.6 12.4 %collective-permute-start = (f32[64,2048]{1,0:T(8,128)S(1)}, f32[64,2048]{1,0:T(8,128)S(1)}, u32[]{:S(2)}, u32[]{:S(2)}) collective-permute-start(f32[64,2048]{1,0:T(8,128)S(1)} %get-tuple-element.186), channel_id=1, source_target_pairs={{0,2},{2,4},{4,6},{6,8},{8,10},{10,12},{12,14},{14,16},{16,18},{18... | collective-permute-start | bytes 1572872 | tf_op jit(solution)/shard_map/while/body/eval_jaxpr/ppermute | solution.py:18
  479.5 13.0 %collective-permute-start.1 = (f32[64,2048]{1,0:T(8,128)S(1)}, f32[64,2048]{1,0:T(8,128)S(1)}, u32[]{:S(2)}, u32[]{:S(2)}) collective-permute-start(f32[64,2048]{1,0:T(8,128)S(1)} %get-tuple-element.187), channel_id=1, source_target_pairs={{2,0},{4,2},{6,4},{8,6},{10,8},{12,10},{14,12},{16,14},{18,16},{20... | collective-permute-start | bytes 1572872 | tf_op jit(solution)/shard_map/while/body/eval_jaxpr/ppermute | solution.py:20
  492.6 4.0 copy-start
  521.6 14.8 %collective-permute-start = (f32[64,2048]{1,0:T(8,128)S(1)}, f32[64,2048]{1,0:T(8,128)S(1)}, u32[]{:S(2)}, u32[]{:S(2)}) collective-permute-start(f32[64,2048]{1,0:T(8,128)S(1)} %get-tuple-element.186), channel_id=1, source_target_pairs={{0,2},{2,4},{4,6},{6,8},{8,10},{10,12},{12,14},{14,16},{16,18},{18... | collective-permute-start | bytes 1572872 | tf_op jit(solution)/shard_map/while/body/eval_jaxpr/ppermute | solution.py:18
  523.5 15.4 %collective-permute-start.1 = (f32[64,2048]{1,0:T(8,128)S(1)}, f32[64,2048]{1,0:T(8,128)S(1)}, u32[]{:S(2)}, u32[]{:S(2)}) collective-permute-start(f32[64,2048]{1,0:T(8,128)S(1)} %get-tuple-element.187), channel_id=1, source_target_pairs={{2,0},{4,2},{6,4},{8,6},{10,8},{12,10},{14,12},{16,14},{18,16},{20... | collective-permute-start | bytes 1572872 | tf_op jit(solution)/shard_map/while/body/eval_jaxpr/ppermute | solution.py:20
  539.0 4.0 copy-start
  568.0 12.4 %collective-permute-start = (f32[64,2048]{1,0:T(8,128)S(1)}, f32[64,2048]{1,0:T(8,128)S(1)}, u32[]{:S(2)}, u32[]{:S(2)}) collective-permute-start(f32[64,2048]{1,0:T(8,128)S(1)} %get-tuple-element.186), channel_id=1, source_target_pairs={{0,2},{2,4},{4,6},{6,8},{8,10},{10,12},{12,14},{14,16},{16,18},{18... | collective-permute-start | bytes 1572872 | tf_op jit(solution)/shard_map/while/body/eval_jaxpr/ppermute | solution.py:18
  569.9 13.0 %collective-permute-start.1 = (f32[64,2048]{1,0:T(8,128)S(1)}, f32[64,2048]{1,0:T(8,128)S(1)}, u32[]{:S(2)}, u32[]{:S(2)}) collective-permute-start(f32[64,2048]{1,0:T(8,128)S(1)} %get-tuple-element.187), channel_id=1, source_target_pairs={{2,0},{4,2},{6,4},{8,6},{10,8},{12,10},{14,12},{16,14},{18,16},{20... | collective-permute-start | bytes 1572872 | tf_op jit(solution)/shard_map/while/body/eval_jaxpr/ppermute | solution.py:20
  583.0 4.0 copy-start
  612.0 14.8 %collective-permute-start = (f32[64,2048]{1,0:T(8,128)S(1)}, f32[64,2048]{1,0:T(8,128)S(1)}, u32[]{:S(2)}, u32[]{:S(2)}) collective-permute-start(f32[64,2048]{1,0:T(8,128)S(1)} %get-tuple-element.186), channel_id=1, source_target_pairs={{0,2},{2,4},{4,6},{6,8},{8,10},{10,12},{12,14},{14,16},{16,18},{18... | collective-permute-start | bytes 1572872 | tf_op jit(solution)/shard_map/while/body/eval_jaxpr/ppermute | solution.py:18
  613.9 15.4 %collective-permute-start.1 = (f32[64,2048]{1,0:T(8,128)S(1)}, f32[64,2048]{1,0:T(8,128)S(1)}, u32[]{:S(2)}, u32[]{:S(2)}) collective-permute-start(f32[64,2048]{1,0:T(8,128)S(1)} %get-tuple-element.187), channel_id=1, source_target_pairs={{2,0},{4,2},{6,4},{8,6},{10,8},{12,10},{14,12},{16,14},{18,16},{20... | collective-permute-start | bytes 1572872 | tf_op jit(solution)/shard_map/while/body/eval_jaxpr/ppermute | solution.py:20
  658.4 12.4 %collective-permute-start = (f32[64,2048]{1,0:T(8,128)S(1)}, f32[64,2048]{1,0:T(8,128)S(1)}, u32[]{:S(2)}, u32[]{:S(2)}) collective-permute-start(f32[64,2048]{1,0:T(8,128)S(1)} %get-tuple-element.186), channel_id=1, source_target_pairs={{0,2},{2,4},{4,6},{6,8},{8,10},{10,12},{12,14},{14,16},{16,18},{18... | collective-permute-start | bytes 1572872 | tf_op jit(solution)/shard_map/while/body/eval_jaxpr/ppermute | solution.py:18
  660.4 13.0 %collective-permute-start.1 = (f32[64,2048]{1,0:T(8,128)S(1)}, f32[64,2048]{1,0:T(8,128)S(1)}, u32[]{:S(2)}, u32[]{:S(2)}) collective-permute-start(f32[64,2048]{1,0:T(8,128)S(1)} %get-tuple-element.187), channel_id=1, source_target_pairs={{2,0},{4,2},{6,4},{8,6},{10,8},{12,10},{14,12},{16,14},{18,16},{20... | collective-permute-start | bytes 1572872 | tf_op jit(solution)/shard_map/while/body/eval_jaxpr/ppermute | solution.py:20
  702.4 14.8 %collective-permute-start = (f32[64,2048]{1,0:T(8,128)S(1)}, f32[64,2048]{1,0:T(8,128)S(1)}, u32[]{:S(2)}, u32[]{:S(2)}) collective-permute-start(f32[64,2048]{1,0:T(8,128)S(1)} %get-tuple-element.186), channel_id=1, source_target_pairs={{0,2},{2,4},{4,6},{6,8},{8,10},{10,12},{12,14},{14,16},{16,18},{18... | collective-permute-start | bytes 1572872 | tf_op jit(solution)/shard_map/while/body/eval_jaxpr/ppermute | solution.py:18
  704.4 15.4 %collective-permute-start.1 = (f32[64,2048]{1,0:T(8,128)S(1)}, f32[64,2048]{1,0:T(8,128)S(1)}, u32[]{:S(2)}, u32[]{:S(2)}) collective-permute-start(f32[64,2048]{1,0:T(8,128)S(1)} %get-tuple-element.187), channel_id=1, source_target_pairs={{2,0},{4,2},{6,4},{8,6},{10,8},{12,10},{14,12},{16,14},{18,16},{20... | collective-permute-start | bytes 1572872 | tf_op jit(solution)/shard_map/while/body/eval_jaxpr/ppermute | solution.py:20
  (4 other events, 16.1 us)
where the time goes:
time: 757 us; the launch traced here: 748 us
  local copies, waits for them, and re-layouts  430 us (57%)
  starting transfers between devices  94.7 us (13%)
  other arithmetic  82.3 us (11%)
  waiting for transfers between devices  78.3 us (10%)
  matrix products  45.1 us (6%)
  loops' own time  13.1 us (2%)
    dynamic_update_slice x16, local copies, waits for them, and re-layouts, apply_sweep(): lax.dynamic_update_slice_in_dim(padded, updated.reshape(length + band_wid...  250 us
    slice x16, local copies, waits for them, and re-layouts, one_round(): return extended[margin:margin + local_rows]  75.2 us
    ppermute x17, waiting for transfers between devices, extended_2(): lax.ppermute(tail, axis, [(i, (i + 1) % count) for i in range(ends)])  74.1 us
    ppermute x17, starting transfers between devices, extended_2(): lax.ppermute(head, axis, [((i + 1) % count, i) for i in range(ends)])  60.7 us
    sub x16, other arithmetic, apply_sweep(): windows - (factor[:, None] * window_vecs)[:, :, None] * project[:, None, :]  54.2 us
    dot_general x16, matrix products, apply_sweep(): jnp.einsum('wr,wrc->wc', window_vecs, windows, precision=lax.Precision.HI...  45.1 us
    while x96, local copies, waits for them, and re-layouts  41.3 us
    ppermute x17, starting transfers between devices, extended_2(): lax.ppermute(tail, axis, [(i, (i + 1) % count) for i in range(ends)])  34 us
  transfers between devices with their start and end apart: 34, of which 18 were waited for; matrix products, arithmetic and copies ran while one was open for 12% of the time, Pallas kernels for 0%

commit v1 on v0

v1 whole, which is shorter than its diff:
```python
import functools

import jax
import jax.numpy as jnp
from jax import lax
from jax.experimental import pallas as pl
from jax.experimental.pallas import tpu as pltpu
from jax.sharding import PartitionSpec as P

WIDTH = 64
SWEEPS = 16
WINDOWS = 8
ROWS = WIDTH * WINDOWS
HALF = ROWS // 2
BAND = 5 * SWEEPS
LOCAL = 7 * SWEEPS
EXTRA = 128
F32 = jnp.float32
BF16 = jnp.bfloat16


def split(a):
    hi = a.astype(BF16)
    return hi, (a - hi.astype(F32)).astype(BF16)


def mm(a, b):
    return jnp.dot(a, b, preferred_element_type=F32)


def mm_nt(a, b):
    return lax.dot_general(a, b, (((1,), (1,)), ((), ())), preferred_element_type=F32)


def mm3(a, b):
    return mm(a[0], b[0]) + mm(a[1], b[0]) + mm(a[0], b[1])


def iota(shape, dim):
    return lax.broadcasted_iota(jnp.int32, shape, dim)


def eliminate(target, column, row, first):
    if first < 7:
        return target - column * row
    lower = target[8:] - column[8:] * row
    return jnp.concatenate([target[:8], lower], axis=0)


def prepare_kernel(x_ref, off_ref, high_ref, low_ref, window_ref, xbuf, off, sems, off_sem):
    count = sems.shape[0]
    size = ROWS // count
    fetch = pltpu.make_async_copy(off_ref, off, off_sem)
    fetch.start()
    copies = []
    for j in range(count):
        rows = pl.ds(j * size, size)
        copies.append(pltpu.make_async_copy(x_ref.at[rows], xbuf.at[rows], sems.at[j]))
        copies[-1].start()
    fetch.wait()
    sweep = iota((SWEEPS, ROWS), 0)
    offset = jnp.zeros((SWEEPS, ROWS), jnp.int32)
    for s in range(SWEEPS):
        offset = jnp.where(sweep == s, off[s], offset)
    window = jnp.right_shift(iota((SWEEPS, ROWS), 1) - offset, 6)
    window_ref[...] = jnp.where((window < 0) & (lax.axis_index("row") == 0), -2, window)
    for j in range(count):
        copies[j].wait()
        rows = slice(j * size, (j + 1) * size)
        high, low = split(xbuf[rows])
        high_ref[rows] = high
        low_ref[rows] = low


def reflector_rows(vector_refs, window_ref):
    vectors = [ref[...] for ref in vector_refs]
    if len(vectors) == 2:
        first = lax.axis_index("col") == 0
        own, other = vectors
        vectors = [jnp.where(first, own, other), jnp.where(first, other, own)]
    refl = jnp.concatenate(vectors, axis=0)
    window = window_ref[...]
    return jnp.concatenate(
        [jnp.where(window == k, refl, 0.0) for k in range(-1, WINDOWS)], axis=0
    )


def halves_of(vt):
    return vt[:BAND, :HALF], vt[-BAND:, HALF:]


def project_kernel(chunk, inputs, *refs):
    window_ref, high_ref, low_ref = refs[inputs : inputs + 3]
    sums_ref, beside_ref, across_ref, down_ref, up_ref, solve_ref = refs[inputs + 3 :]
    columns = high_ref.shape[1]
    is_even = lax.rem(lax.axis_index("row"), 2) == 0
    vt = reflector_rows(refs[:inputs], window_ref)

    def send(cut, down, up):
        down_ref[:, cut] = down
        up_ref[:, cut] = up
        beside_ref[:, cut] = jnp.where(is_even, up[:8], down[:8])
        across_ref[:, cut] = jnp.where(is_even, down[:8], up[:8])

    tau = 2.0 / jnp.sum(vt[SWEEPS:-SWEEPS] * vt[SWEEPS:-SWEEPS], axis=1, keepdims=True)
    halves = [split(v) for v in halves_of(vt)]
    grams = [mm_nt(h, h) + mm_nt(l, h) + mm_nt(h, l) for h, l in halves]

    strict = iota((SWEEPS, BAND), 1) % SWEEPS < iota((SWEEPS, BAND), 0)

    def gram(k, shift):
        row = (k + 1) * SWEEPS
        if k < 3:
            return grams[0][row : row + SWEEPS], (k + 1 + shift) * SWEEPS
        row -= 4 * SWEEPS
        return grams[1][row : row + SWEEPS], (k - 3 + shift) * SWEEPS

    def strict_columns(k, shift, scale):
        block, base = gram(k, shift)
        if k == 3 and shift == 0:
            both = grams[0][4 * SWEEPS :, 4 * SWEEPS :] + grams[1][:SWEEPS, :SWEEPS]
            block, base = both, 0
        block = jnp.where(strict[:, : block.shape[1]], block, 0.0)
        if scale is not None:
            block = block * scale
        return lambda s: block[:, base + s : base + s + 1]

    tall = [jnp.concatenate([h, l], axis=0) for h, l in halves]
    chunks = columns // chunk

    def project(j):
        cut = slice(j * chunk, (j + 1) * chunk)
        sums = []
        for part in range(2):
            rows = slice(part * HALF, (part + 1) * HALF)
            both = mm(tall[part], high_ref[rows, cut])
            sums.append(both[:BAND] + both[BAND:] + mm(halves[part][0], low_ref[rows, cut]))
        shared = sums[0][-SWEEPS:] + sums[1][:SWEEPS]
        sums_ref[: 3 * SWEEPS, cut] = sums[0][SWEEPS:-SWEEPS]
        sums_ref[3 * SWEEPS : 4 * SWEEPS, cut] = shared
        sums_ref[4 * SWEEPS :, cut] = sums[1][SWEEPS:-SWEEPS]
        down_ref[:, cut] = sums[0][:SWEEPS]
        up_ref[:, cut] = sums[1][-SWEEPS:]

    lane = iota((SWEEPS, 128), 1)
    sub = iota((SWEEPS, 128), 0)
    state = []
    inner, outer = [], []
    for k in range(WINDOWS):
        here = lane == sub + k * SWEEPS
        if k < WINDOWS - 1:
            scale = tau[k * SWEEPS : (k + 1) * SWEEPS]
            state.append(jnp.where(here, scale, 0.0))
            inner.append(strict_columns(k, 0, scale))
            outer.append(strict_columns(k, 1, scale))
        else:
            state.append(jnp.where(here, 1.0, 0.0))
    leave = jnp.zeros((SWEEPS, 128), F32)
    leaving = strict_columns(-1, 1, None)
    for s in range(SWEEPS - 1):
        for j in range(s * chunks // (SWEEPS - 1), (s + 1) * chunks // (SWEEPS - 1)):
            project(j)
        rows = [state[k][s : s + 1] for k in range(WINDOWS)]
        for k in range(WINDOWS - 1):
            state[k] = eliminate(state[k], inner[k](s), rows[k], s)
            state[k] = eliminate(state[k], outer[k](s), rows[k + 1], s)
        leave = eliminate(leave, leaving(s), rows[0], s)

    solve = jnp.concatenate(state[: WINDOWS - 1], axis=0)
    solve_ref[...] = solve
    pass_on = split(leave[:, :LOCAL])

    bottom = jnp.concatenate([grams[0][:SWEEPS], jnp.zeros((SWEEPS, 128 - BAND), F32)], axis=1)
    top = jnp.concatenate([grams[1][-SWEEPS:], jnp.zeros((SWEEPS, 128 - BAND), F32)], axis=1)
    top = jnp.where(lane < SWEEPS, pltpu.roll(top, 128 - 4 * SWEEPS, 1), 0.0)
    response = pltpu.roll(leave, 2 * SWEEPS, 1)
    side = jnp.where(lane < SWEEPS, bottom, jnp.where(lane < 2 * SWEEPS, response, 0.0))
    send(slice(columns, columns + EXTRA), side, top)

    pass_tall = jnp.concatenate(pass_on, axis=0)
    for j in range(chunks):
        cut = slice(j * chunk, (j + 1) * chunk)
        high, low = split(sums_ref[:, cut])
        both = mm(pass_tall, high)
        leaving = both[:SWEEPS] + both[SWEEPS:] + mm(pass_on[0], low)
        send(cut, down_ref[:, cut] + leaving, up_ref[:, cut])


def bands_of(first, local, last):
    return (
        jnp.concatenate([first, local[: 4 * SWEEPS]], axis=0),
        jnp.concatenate([local[3 * SWEEPS :], last], axis=0),
    )


def stack(a):
    high, low = split(a)
    return jnp.concatenate([high, high, low], axis=0)


def straddling(gram, base):
    size = gram.shape[0]
    lane, sub = iota((size, 128), 1), iota((size, 128), 0)
    squares = jnp.sum(jnp.where(sub == lane, gram, 0.0), axis=1, keepdims=True)
    tau = jnp.where(squares > 0.0, 2.0 / squares, 0.0)
    strict = jnp.where(lane < sub, gram, 0.0) * tau
    return tau, strict, jnp.where(lane == sub + base, tau, 0.0)


def complete_kernel(parity, down_ref, up_ref, got_ref, *refs):
    send_refs = [ref for ref in refs if ref.shape[0] == 8]
    columns = down_ref.shape[1] - EXTRA
    row, count = lax.axis_index("row"), lax.axis_size("row")
    ours = lax.rem(row, 2) == parity

    def got(cut):
        return jnp.where(row < count - 1, got_ref[:, cut], 0.0)

    side = slice(columns, columns + EXTRA)
    own_side = down_ref[8:, side]
    _, strict, solve = straddling(up_ref[:8, side] + got(side), 0)
    carry = jnp.zeros((8, 128), F32)
    for s in range(8):
        row_s = solve[s : s + 1]
        carry = carry + own_side[:, SWEEPS + s : SWEEPS + s + 1] * row_s
        if s < 7:
            solve = solve - strict[:, s : s + 1] * row_s
    begin = 0
    for send_ref in send_refs:
        for place in range(0, send_ref.shape[1], 128):
            cut = slice(begin + place, begin + place + 128)
            down = down_ref[8:, cut]
            if cut.start < columns:
                below = up_ref[:8, cut] + got(cut)
                for s in range(8):
                    down = down + carry[:, s : s + 1] * below[s : s + 1]
            send_ref[:, place : place + 128] = jnp.where(ours, down, up_ref[8:, cut])
        begin += send_ref.shape[1]


def subtract_inside(chunk, begin, high_ref, low_ref, sums_ref, cols_ref, solve, inner_ref):
    solve = split(solve[:, :LOCAL])
    solve_tall = jnp.concatenate(solve, axis=0)
    none = jnp.zeros((SWEEPS, chunk), F32)
    for j in range(inner_ref.shape[1] // chunk):
        put = slice(j * chunk, (j + 1) * chunk)
        cut = slice(begin + j * chunk, begin + (j + 1) * chunk)
        high, low = split(sums_ref[:, cut])
        both = mm(solve_tall, high)
        coeff = both[:LOCAL] + both[LOCAL:] + mm(solve[0], low)
        for part, band in enumerate(bands_of(none, coeff, none)):
            rows = slice(part * HALF, (part + 1) * HALF)
            slab = high_ref[rows, cut].astype(F32) + low_ref[rows, cut].astype(F32)
            inner_ref[rows, put] = slab - mm(cols_ref[rows, :], stack(band))


def inside_kernel(chunk, inputs, *refs):
    window_ref, high_ref, low_ref, sums_ref, solve_ref, _ = refs[inputs : inputs + 6]
    inner_ref, ends_ref, cols_ref = refs[inputs + 6 :]
    for part, v in enumerate(halves_of(reflector_rows(refs[:inputs], window_ref))):
        high, low = (a.astype(F32) for a in split(v))
        tall = jnp.concatenate([high, low, high], axis=0)
        cols_ref[part * HALF : (part + 1) * HALF, :] = jnp.transpose(tall).astype(BF16)
    solve = solve_ref[...]
    lane = iota((LOCAL, 128), 1)
    spread = jnp.zeros((LOCAL, 128), F32)
    for group in range(3):
        begin = 2 * SWEEPS * group + SWEEPS
        moved = pltpu.roll(solve, SWEEPS + begin, 1)
        spread = jnp.where((lane >= begin) & (lane < begin + SWEEPS), moved, spread)
    lane, sub = iota((SWEEPS, 128), 1), iota((SWEEPS, 128), 0)
    used = lane < 6 * SWEEPS
    first = jnp.where((lane % (2 * SWEEPS) == sub) & used, 1.0, 0.0)
    last = jnp.where((lane % (2 * SWEEPS) == sub + SWEEPS) & used, 1.0, 0.0)
    for part, band in enumerate(bands_of(first, spread, last)):
        rows = slice(part * HALF, (part + 1) * HALF)
        high, low = split(mm(cols_ref[rows, :], stack(band)))
        group = iota((HALF, 128), 1) // (2 * SWEEPS)
        ends_ref[rows, :] = jnp.where(group == 1, low.astype(F32), high.astype(F32)).astype(BF16)

    subtract_inside(chunk, 0, high_ref, low_ref, sums_ref, cols_ref, solve, inner_ref)


def inside_more_kernel(chunk, high_ref, low_ref, sums_ref, solve_ref, cols_ref, inner_ref):
    begin = high_ref.shape[1] - inner_ref.shape[1]
    subtract_inside(chunk, begin, high_ref, low_ref, sums_ref, cols_ref, solve_ref[...], inner_ref)


def finish_kernel(chunk, *refs):
    across_refs, beside_refs, refs = refs[:2], refs[2:5], refs[5:]
    down_ref, up_ref, ends_ref = refs[:3]
    inner_refs, (out_ref, obuf, coeff_ref, sems) = refs[3:5], refs[5:]
    columns = 2 * inner_refs[0].shape[1]
    row, count = lax.axis_index("row"), lax.axis_size("row")
    is_even = lax.rem(row, 2) == 0

    def messages(cut):
        across = jnp.concatenate([ref[:, cut] for ref in across_refs], axis=0)
        across = jnp.where((row > 0) & (row < count - 1), across, 0.0)
        first, left, right = beside_refs
        middle = left.shape[1]
        if cut.start < middle:
            last = left[:, cut]
        else:
            last = right[:, cut.start - middle : cut.stop - middle]
        beside = jnp.concatenate([first[:, cut], last], axis=0)
        below = jnp.where(is_even, beside, across)
        above = jnp.where(is_even, across, beside)
        return down_ref[:, cut], up_ref[:, cut], below, above

    own_side, own_top, next_side, prev_top = messages(slice(columns, columns + EXTRA))
    _, n7, c7 = straddling(own_top + next_side, 0)
    tau1, n1, c1 = straddling(prev_top + own_side, SWEEPS)
    e1 = own_side * tau1
    for s in range(SWEEPS - 1):
        row7, row1 = c7[s : s + 1], c1[s : s + 1]
        c7 = eliminate(c7, n7[:, s : s + 1], row7, s)
        c1 = eliminate(c1, n1[:, s : s + 1], row1, s)
        c1 = eliminate(c1, -e1[:, SWEEPS + s : SWEEPS + s + 1], row7, s)
    join = split(jnp.concatenate([c1, c7], axis=0)[:, : 2 * SWEEPS])
    effect = ends_ref[:, : 6 * SWEEPS]

    for j in range(columns // chunk):
        cut = slice(j * chunk, (j + 1) * chunk)
        down, up, below, above = messages(cut)
        incoming = jnp.concatenate([up + below, down + above], axis=0)
        coeff_ref[:, cut] = stack(mm3(join, split(incoming)))

    stores = []
    for j in range(columns // chunk):
        cut = slice(j * chunk, (j + 1) * chunk)
        part, place = divmod(j * chunk, columns // 2)
        inner = inner_refs[part][:, place : place + chunk]
        obuf[:, cut] = inner - mm(effect, coeff_ref[:, cut])
        cut = pl.ds(j * chunk, chunk)
        stores.append(pltpu.make_async_copy(obuf.at[:, cut], out_ref.at[:, cut], sems.at[j]))
        stores[-1].start(priority=j % 2)
    for store in stores:
        store.wait()


def in_hbm(a):
    return pltpu.with_memory_space_constraint(a, pltpu.HBM)


def local(eig_slab, reflectors, row_offsets):
    rows, columns = eig_slab.shape
    assert rows == ROWS and columns % 256 == 0
    chunk = 256 if columns % 512 == 0 else 128
    chunks = columns // chunk
    count = lax.axis_size("row")
    groups = lax.axis_size("col")
    vmem = pl.BlockSpec(memory_space=pltpu.VMEM)
    hbm = pl.BlockSpec(memory_space=pltpu.HBM)
    params = pltpu.CompilerParams(vmem_limit_bytes=16 * 1024 * 1024)
    shape = jax.ShapeDtypeStruct
    slab_bytes = rows * columns * 4

    def cost(passes, flops):
        return pl.CostEstimate(flops=flops, bytes_accessed=passes * slab_bytes, transcendentals=0)

    if groups == 2:
        vectors = (reflectors, lax.ppermute(reflectors, "col", [(0, 1), (1, 0)]))
    elif groups == 1:
        vectors = (reflectors,)
    else:
        vectors = (lax.all_gather(reflectors, "col", axis=0, tiled=True),)

    high, low, window = pl.pallas_call(
        prepare_kernel,
        out_shape=(
            shape((rows, columns), BF16),
            shape((rows, columns), BF16),
            shape((SWEEPS, rows), jnp.int32),
        ),
        in_specs=[hbm, hbm],
        out_specs=(vmem,) * 3,
        scratch_shapes=[
            pltpu.VMEM((rows, columns), F32),
            pltpu.SMEM((SWEEPS,), jnp.int32),
            pltpu.SemaphoreType.DMA((8,)),
            pltpu.SemaphoreType.DMA(()),
        ],
        compiler_params=params,
        cost_estimate=cost(2, 0),
        name="prepare",
    )(in_hbm(eig_slab), in_hbm(row_offsets))

    own = shape((SWEEPS, columns + EXTRA), F32)
    eight = shape((8, columns + EXTRA), F32)
    sums, beside, across, down, up, solve = pl.pallas_call(
        functools.partial(project_kernel, chunk, len(vectors)),
        out_shape=(
            shape((LOCAL, columns), F32),
            eight,
            eight,
            own,
            own,
            shape((LOCAL, 128), F32),
        ),
        in_specs=[vmem] * (len(vectors) + 3),
        out_specs=(vmem,) * 6,
        compiler_params=params,
        cost_estimate=cost(2, rows * columns * 240),
        name="project",
    )(*vectors, window, high, low)

    pairs = [(i, i + 1) for i in range(0, count, 2)]
    on_chip = pairs + [(j, i) for i, j in pairs]
    pairs = [
        (i * groups + c, (i + 1) * groups + c)
        for i in range(1, count - 1, 2)
        for c in range(groups)
    ]
    pairs += [
        (i * groups + c, i * groups + c + 1)
        for i in (0, count - 1)
        for c in range(0, groups - 1, 2)
    ]
    over_chips = pairs + [(j, i) for i, j in pairs]

    got_beside = lax.ppermute(beside, "row", on_chip)
    got_across = lax.ppermute(across, ("row", "col"), over_chips)
    late = pl.pallas_call(
        functools.partial(complete_kernel, 0),
        out_shape=eight,
        in_specs=[vmem] * 3,
        out_specs=vmem,
        compiler_params=params,
        name="complete_even",
    )(down, up, got_beside)
    got_late = lax.ppermute(late, ("row", "col"), over_chips)

    half = shape((rows, columns // 2), F32)
    inner, ends, cols = pl.pallas_call(
        functools.partial(inside_kernel, chunk, len(vectors)),
        out_shape=(half, shape((rows, 128), BF16), shape((rows, 3 * BAND), BF16)),
        in_specs=[vmem] * (len(vectors) + 6),
        out_specs=(vmem,) * 3,
        compiler_params=params,
        cost_estimate=cost(2, rows * columns * 240),
        name="inside",
    )(*vectors, window, high, low, sums, solve, late)

    latest = pl.pallas_call(
        functools.partial(complete_kernel, 1),
        out_shape=(shape((8, columns // 2), F32), shape((8, columns // 2 + EXTRA), F32)),
        in_specs=[vmem] * 4,
        out_specs=(vmem,) * 2,
        compiler_params=params,
        name="complete_odd",
    )(down, up, got_across, ends)
    got_latest = [lax.ppermute(part, "row", on_chip) for part in latest]

    more = pl.pallas_call(
        functools.partial(inside_more_kernel, chunk),
        out_shape=half,
        in_specs=[vmem] * 5,
        out_specs=vmem,
        compiler_params=params,
        cost_estimate=cost(2, rows * columns * 240),
        name="inside_more",
    )(high, low, sums, solve, cols)

    return pl.pallas_call(
        functools.partial(finish_kernel, chunk),
        out_shape=shape((rows, columns), F32),
        in_specs=[vmem] * 10,
        out_specs=hbm,
        scratch_shapes=[
            pltpu.VMEM((rows, columns), F32),
            pltpu.VMEM((6 * SWEEPS, columns), BF16),
            pltpu.SemaphoreType.DMA((chunks,)),
        ],
        compiler_params=params,
        cost_estimate=cost(2, rows * columns * 200),
        name="finish",
    )(got_across, got_late, got_beside, *got_latest, down, up, ends, inner, more)


def solution(mesh):
    placed = (P("row", "col"), P("col", "row"), P())
    return jax.shard_map(
        local, mesh=mesh, in_specs=placed, out_specs=P("row", "col"), check_vma=False
    )
```

time: 757 us -> 16.2 us (0.02)
  the two profiles are of different devices: /device:TPU:10 before, /device:TPU:0 now
where the time goes in v1:
time: 16.2 us; the launch traced here: 16.1 us
  Pallas kernels  9.47 us (58%)
  starting transfers between devices  6.5 us (40%)
    ppermute x1, starting transfers between devices, local(): vectors = (reflectors, lax.ppermute(reflectors, 'col', [(0, 1), (1, 0)]))  2.97 us
    pallas_call x1, Pallas kernels, local(): pl.pallas_call(functools.partial(finish_kernel, chunk), out_shape=shape((...  2.8 us
    pallas_call x1, Pallas kernels, local(): pl.pallas_call(prepare_kernel, out_shape=(shape((rows, columns), BF16), s...  2.32 us
    ppermute x1, starting transfers between devices, local(): got_across = lax.ppermute(across, ('row', 'col'), over_chips)  1.66 us
    pallas_call x1, Pallas kernels, local(): pl.pallas_call(functools.partial(inside_kernel, chunk, len(vectors)), out...  1.39 us
    ppermute x1, starting transfers between devices, local(): got_late = lax.ppermute(late, ('row', 'col'), over_chips)  1.24 us
    pallas_call x1, Pallas kernels, local(): pl.pallas_call(functools.partial(project_kernel, chunk, len(vectors)), ou...  1.22 us
    pallas_call x1, Pallas kernels, local(): pl.pallas_call(functools.partial(inside_more_kernel, chunk), out_shape=ha...  1.13 us
  transfers between devices with their start and end apart: 6, of which 0 were waited for; matrix products, arithmetic and copies ran while one was open for 0% of the time, Pallas kernels for 34%

profile of v1, /device:TPU:0, one launch (start us, length us, event | category | flops | bytes accessed | tf_op | source)
XLA Modules:
  0.0 16.1 jit_solution(2595922275464217223)
XLA Ops:
  0.0 0.0 copy-start
  0.0 3.0 %collective-permute-start = (f32[8,512]{1,0:T(8,128)}, f32[8,512]{1,0:T(8,128)S(1)}, u32[]{:S(2)}, u32[]{:S(2)}) collective-permute-start(f32[8,512]{1,0:T(8,128)} %refs_0_.3), channel_id=1, source_target_pairs={{0,1},{1,0},{2,3},{3,2},{4,5},{5,4},{6,7},{7,6},{8,9},{9,8},{10,11... | collective-permute-start | bytes 49160 | tf_op jit(solution)/shard_map/ppermute | solution.py:363
  3.0 2.3 %prepare.1 = (bf16[512,2048]{1,0:T(8,128)(2,1)S(1)}, bf16[512,2048]{1,0:T(8,128)(2,1)S(1)}, s32[16,512]{1,0:T(8,128)S(1)}) custom-call(f32[512,2048]{1,0:T(8,128)} %x_ref.1, s32[16]{0:T(128)} %off_ref.1), custom_call_target="tpu_custom_call" | custom-call | bytes 8388608 | tf_op jit(solution)/shard_map/prepare/pallas_call | solution.py:369
  5.3 0.0 collective-permute-done.refs_1_
  5.3 0.0 copy-done
  5.3 1.2 %project.1 = (f32[112,2048]{1,0:T(8,128)S(1)}, f32[8,2176]{1,0:T(8,128)S(1)}, f32[8,2176]{1,0:T(8,128)S(1)}, f32[16,2176]{1,0:T(8,128)S(1)}, f32[16,2176]{1,0:T(8,128)S(1)}, /*index=5*/f32[112,128]{1,0:T(8,128)S(1)}) custom-call(f32[8,512]{1,0:T(8,128)S(1)} %copy-done, f32[8,512]{1,0:T(8,128)S(1)} %collective-permute-done.refs_1_, ...), custom_call_target="tpu_custom_call" | custom-call | flops 251658240 | bytes 8388608 | tf_op jit(solution)/shard_map/project/pallas_call | solution.py:391
  6.5 0.1 collective-permute-start.2
  6.6 1.7 %collective-permute-start.1 = (f32[8,2176]{1,0:T(8,128)S(1)}, f32[8,2176]{1,0:T(8,128)S(1)}, u32[]{:S(2)}, u32[]{:S(2)}) collective-permute-start(f32[8,2176]{1,0:T(8,128)S(1)} %get-tuple-element.22), channel_id=1, source_target_pairs={{2,4},{3,5},{6,8},{7,9},{10,12},{11,13},{14,16},{15,17},{18,20},{1... | collective-permute-start | bytes 208904 | tf_op jit(solution)/shard_map/ppermute | solution.py:423
  8.3 0.0 collective-permute-done.2.got_ref.refs_2_
  8.3 0.3 %complete_even.1.refs_7_ = f32[8,2176]{1,0:T(8,128)S(1)} custom-call(f32[16,2176]{1,0:T(8,128)S(1)} %get-tuple-element.23.down_ref.refs_5_, f32[16,2176]{1,0:T(8,128)S(1)} %get-tuple-element.24.up_ref.refs_6_, f32[8,2176]{1,0:T(8,128)S(1)} %collective-permute-done.2.got_ref.refs_2_), custom_call_target="tpu_custom_call" | custom-call | tf_op jit(solution)/shard_map/complete_even/pallas_call | solution.py:424
  8.6 1.2 %collective-permute-start.3 = (f32[8,2176]{1,0:T(8,128)S(1)}, f32[8,2176]{1,0:T(8,128)S(1)}, u32[]{:S(2)}, u32[]{:S(2)}) collective-permute-start(f32[8,2176]{1,0:T(8,128)S(1)} %complete_even.1.refs_7_), channel_id=1, source_target_pairs={{2,4},{3,5},{6,8},{7,9},{10,12},{11,13},{14,16},{15,17},{18,20},{1... | collective-permute-start | bytes 208904 | tf_op jit(solution)/shard_map/ppermute | solution.py:432
  9.8 1.4 %inside.1 = (f32[512,1024]{1,0:T(8,128)S(1)}, bf16[512,128]{1,0:T(8,128)(2,1)S(1)}, bf16[512,240]{1,0:T(8,128)(2,1)S(1)}) custom-call(f32[8,512]{1,0:T(8,128)S(1)} %copy-done, f32[8,512]{1,0:T(8,128)S(1)} %collective-permute-done.refs_1_, s32[16,512]{1,0:T(8,128)S(1)} %get-tuple-element.19.refs_2_, bf16[512,2048]{1,0:T(8,128)(2,1)S(1)} %get-tuple-element.20.refs_3_.high_ref, ...), custom_call_target="tpu_custom_call" | custom-call | flops 251658240 | bytes 8388608 | tf_op jit(solution)/shard_map/inside/pallas_call | solution.py:435
  11.2 0.0 collective-permute-done.1.got_ref.refs_0_
  11.2 0.3 %complete_odd.1 = (f32[8,1024]{1,0:T(8,128)S(1)}, f32[8,1152]{1,0:T(8,128)S(1)}) custom-call(f32[16,2176]{1,0:T(8,128)S(1)} %get-tuple-element.23.down_ref.refs_5_, f32[16,2176]{1,0:T(8,128)S(1)} %get-tuple-element.24.up_ref.refs_6_, f32[8,2176]{1,0:T(8,128)S(1)} %collective-permute-done.1.got_ref.refs_0_, bf16[512,128]{1,0:T(8,128)(2,1)S(1)} %get-tuple-element.28.refs_0_.refs_7_), custom_call_target="tpu_custom_call" | custom-call | tf_op jit(solution)/shard_map/complete_odd/pallas_call | solution.py:445
  11.5 0.2 collective-permute-start.5
  11.7 0.4 %collective-permute-start.4 = (f32[8,1024]{1,0:T(8,128)S(1)}, f32[8,1024]{1,0:T(8,128)S(1)}, u32[]{:S(2)}, u32[]{:S(2)}) collective-permute-start(f32[8,1024]{1,0:T(8,128)S(1)} %get-tuple-element.29), channel_id=1, source_target_pairs={{0,2},{4,6},{8,10},{12,14},{16,18},{20,22},{24,26},{28,30},{2,0},{... | collective-permute-start | bytes 98312 | tf_op jit(solution)/shard_map/ppermute | solution.py:453
  12.1 1.1 %inside_more.1.refs_9_ = f32[512,1024]{1,0:T(8,128)S(1)} custom-call(bf16[512,2048]{1,0:T(8,128)(2,1)S(1)} %get-tuple-element.20.refs_3_.high_ref, bf16[512,2048]{1,0:T(8,128)(2,1)S(1)} %get-tuple-element.21.refs_4_.low_ref, f32[112,2048]{1,0:T(8,128)S(1)} %get-tuple-element.26.refs_5_.sums_ref, f32[112,128]{1,0:T(8,128)S(1)} %get-tuple-element.27.refs_6_.solve_ref, ...), custom_call_target="tpu_custom_call" | custom-call | flops 251658240 | bytes 8388608 | tf_op jit(solution)/shard_map/inside_more/pallas_call | solution.py:455
  13.3 0.0 collective-permute-done.4.refs_3_
  13.3 0.0 collective-permute-done.5.refs_4_
  13.3 0.0 collective-permute-done.3.refs_1_
  13.3 2.8 %finish.1 = f32[512,2048]{1,0:T(8,128)} custom-call(f32[8,2176]{1,0:T(8,128)S(1)} %collective-permute-done.1.got_ref.refs_0_, f32[8,2176]{1,0:T(8,128)S(1)} %collective-permute-done.3.refs_1_, f32[8,2176]{1,0:T(8,128)S(1)} %collective-permute-done.2.got_ref.refs_2_, f32[8,1024]{1,0:T(8,128)S(1)} %collective-permute-done.4.refs_3_, ...), custom_call_target="tpu_custom_call" | custom-call | flops 209715200 | bytes 8388608 | tf_op jit(solution)/shard_map/finish/pallas_call | solution.py:465
Async XLA Ops:
  0.0 5.3 %copy-start = (f32[8,512]{1,0:T(8,128)S(1)}, f32[8,512]{1,0:T(8,128)}, u32[]{:S(2)}) copy-start(f32[8,512]{1,0:T(8,128)} %refs_0_.3) | copy-start | bytes 49156
  0.0 5.3 %collective-permute-start = (f32[8,512]{1,0:T(8,128)}, f32[8,512]{1,0:T(8,128)S(1)}, u32[]{:S(2)}, u32[]{:S(2)}) collective-permute-start(f32[8,512]{1,0:T(8,128)} %refs_0_.3), channel_id=1, source_target_pairs={{0,1},{1,0},{2,3},{3,2},{4,5},{5,4},{6,7},{7,6},{8,9},{9,8},{10,11... | collective-permute-start | bytes 49160 | tf_op jit(solution)/shard_map/ppermute | solution.py:363
  6.5 1.7 %collective-permute-start.2 = (f32[8,2176]{1,0:T(8,128)S(1)}, f32[8,2176]{1,0:T(8,128)S(1)}, u32[]{:S(2)}, u32[]{:S(2)}) collective-permute-start(f32[8,2176]{1,0:T(8,128)S(1)} %get-tuple-element.25), channel_id=1, source_target_pairs={{0,2},{4,6},{8,10},{12,14},{16,18},{20,22},{24,26},{28,30},{2,0},{... | collective-permute-start | bytes 208904 | tf_op jit(solution)/shard_map/ppermute | solution.py:422
  6.6 4.6 %collective-permute-start.1 = (f32[8,2176]{1,0:T(8,128)S(1)}, f32[8,2176]{1,0:T(8,128)S(1)}, u32[]{:S(2)}, u32[]{:S(2)}) collective-permute-start(f32[8,2176]{1,0:T(8,128)S(1)} %get-tuple-element.22), channel_id=1, source_target_pairs={{2,4},{3,5},{6,8},{7,9},{10,12},{11,13},{14,16},{15,17},{18,20},{1... | collective-permute-start | bytes 208904 | tf_op jit(solution)/shard_map/ppermute | solution.py:423
  8.6 4.7 %collective-permute-start.3 = (f32[8,2176]{1,0:T(8,128)S(1)}, f32[8,2176]{1,0:T(8,128)S(1)}, u32[]{:S(2)}, u32[]{:S(2)}) collective-permute-start(f32[8,2176]{1,0:T(8,128)S(1)} %complete_even.1.refs_7_), channel_id=1, source_target_pairs={{2,4},{3,5},{6,8},{7,9},{10,12},{11,13},{14,16},{15,17},{18,20},{1... | collective-permute-start | bytes 208904 | tf_op jit(solution)/shard_map/ppermute | solution.py:432
  11.5 1.7 %collective-permute-start.5 = (f32[8,1152]{1,0:T(8,128)S(1)}, f32[8,1152]{1,0:T(8,128)S(1)}, u32[]{:S(2)}, u32[]{:S(2)}) collective-permute-start(f32[8,1152]{1,0:T(8,128)S(1)} %get-tuple-element.30), channel_id=1, source_target_pairs={{0,2},{4,6},{8,10},{12,14},{16,18},{20,22},{24,26},{28,30},{2,0},{... | collective-permute-start | bytes 110600 | tf_op jit(solution)/shard_map/ppermute | solution.py:453
  11.7 1.6 %collective-permute-start.4 = (f32[8,1024]{1,0:T(8,128)S(1)}, f32[8,1024]{1,0:T(8,128)S(1)}, u32[]{:S(2)}, u32[]{:S(2)}) collective-permute-start(f32[8,1024]{1,0:T(8,128)S(1)} %get-tuple-element.29), channel_id=1, source_target_pairs={{0,2},{4,6},{8,10},{12,14},{16,18},{20,22},{24,26},{28,30},{2,0},{... | collective-permute-start | bytes 98312 | tf_op jit(solution)/shard_map/ppermute | solution.py:453

commit v2 on v1

--- a/solution.py
+++ b/solution.py
@@ -34,6 +34,25 @@
 
 def mm3(a, b):
     return mm(a[0], b[0]) + mm(a[1], b[0]) + mm(a[0], b[1])
+
+
+def left_pair(a):
+    high, low = split(a)
+    upper = jnp.concatenate([high, high], axis=1)
+    lower = jnp.concatenate([low, jnp.zeros_like(low)], axis=1)
+    return jnp.concatenate([upper, lower], axis=0)
+
+
+def right_pair(a):
+    high, low = split(a)
+    none = jnp.zeros((128 - a.shape[0], a.shape[1]), BF16)
+    return jnp.concatenate([high, none, low, none], axis=0)
+
+
+def mm_pair(left, right):
+    both = mm(left, right)
+    half = left.shape[0] // 2
+    return both[:half] + both[half:]
 
 
 def iota(shape, dim):
@@ -168,21 +187,27 @@
 
     solve = jnp.concatenate(state[: WINDOWS - 1], axis=0)
     solve_ref[...] = solve
-    pass_on = split(leave[:, :LOCAL])
+    pass_on = left_pair(leave)
 
     bottom = jnp.concatenate([grams[0][:SWEEPS], jnp.zeros((SWEEPS, 128 - BAND), F32)], axis=1)
     top = jnp.concatenate([grams[1][-SWEEPS:], jnp.zeros((SWEEPS, 128 - BAND), F32)], axis=1)
     top = jnp.where(lane < SWEEPS, pltpu.roll(top, 128 - 4 * SWEEPS, 1), 0.0)
     response = pltpu.roll(leave, 2 * SWEEPS, 1)
     side = jnp.where(lane < SWEEPS, bottom, jnp.where(lane < 2 * SWEEPS, response, 0.0))
-    send(slice(columns, columns + EXTRA), side, top)
-
-    pass_tall = jnp.concatenate(pass_on, axis=0)
+    extra = slice(columns, columns + EXTRA)
+    down_ref[:, extra] = side
+    up_ref[:, extra] = top
+
+    def fold(a):
+        return jnp.where(lane[:8] < SWEEPS, a[:8], pltpu.roll(a[8:], 2 * SWEEPS, 1))
+
+    bottom, top = fold(bottom), fold(top)
+    beside_ref[:, extra] = jnp.where(is_even, top, bottom)
+    across_ref[:, extra] = jnp.where(is_even, bottom, top)
+
     for j in range(chunks):
         cut = slice(j * chunk, (j + 1) * chunk)
-        high, low = split(sums_ref[:, cut])
-        both = mm(pass_tall, high)
-        leaving = both[:SWEEPS] + both[SWEEPS:] + mm(pass_on[0], low)
+        leaving = mm_pair(pass_on, right_pair(sums_ref[:, cut]))
         send(cut, down_ref[:, cut] + leaving, up_ref[:, cut])
 
 
@@ -208,7 +233,7 @@
 
 
 def complete_kernel(parity, down_ref, up_ref, got_ref, *refs):
-    send_refs = [ref for ref in refs if ref.shape[0] == 8]
+    send_ref = refs[-1]
     columns = down_ref.shape[1] - EXTRA
     row, count = lax.axis_index("row"), lax.axis_size("row")
     ours = lax.rem(row, 2) == parity
@@ -225,33 +250,32 @@
         carry = carry + own_side[:, SWEEPS + s : SWEEPS + s + 1] * row_s
         if s < 7:
             solve = solve - strict[:, s : s + 1] * row_s
-    begin = 0
-    for send_ref in send_refs:
-        for place in range(0, send_ref.shape[1], 128):
-            cut = slice(begin + place, begin + place + 128)
-            down = down_ref[8:, cut]
-            if cut.start < columns:
-                below = up_ref[:8, cut] + got(cut)
-                for s in range(8):
-                    down = down + carry[:, s : s + 1] * below[s : s + 1]
-            send_ref[:, place : place + 128] = jnp.where(ours, down, up_ref[8:, cut])
-        begin += send_ref.shape[1]
+    for place in range(0, columns, 128):
+        cut = slice(place, place + 128)
+        down = down_ref[8:, cut]
+        below = up_ref[:8, cut] + got(cut)
+        for s in range(8):
+            down = down + carry[:, s : s + 1] * below[s : s + 1]
+        send_ref[:, cut] = jnp.where(ours, down, up_ref[8:, cut])
+    if send_ref.shape[1] > columns:
+        send_ref[:, side] = jnp.zeros((8, EXTRA), F32)
+
+
+def local_part(cut, high_ref, low_ref, sums_ref, cols_ref, solve):
+    coeff = mm_pair(solve, right_pair(sums_ref[:, cut]))
+    none = jnp.zeros((SWEEPS, coeff.shape[1]), F32)
+    for part, band in enumerate(bands_of(none, coeff, none)):
+        rows = slice(part * HALF, (part + 1) * HALF)
+        slab = high_ref[rows, cut].astype(F32) + low_ref[rows, cut].astype(F32)
+        yield rows, slab - mm(cols_ref[rows, :], stack(band))
 
 
 def subtract_inside(chunk, begin, high_ref, low_ref, sums_ref, cols_ref, solve, inner_ref):
-    solve = split(solve[:, :LOCAL])
-    solve_tall = jnp.concatenate(solve, axis=0)
-    none = jnp.zeros((SWEEPS, chunk), F32)
-    for j in range(inner_ref.shape[1] // chunk):
-        put = slice(j * chunk, (j + 1) * chunk)
-        cut = slice(begin + j * chunk, begin + (j + 1) * chunk)
-        high, low = split(sums_ref[:, cut])
-        both = mm(solve_tall, high)
-        coeff = both[:LOCAL] + both[LOCAL:] + mm(solve[0], low)
-        for part, band in enumerate(bands_of(none, coeff, none)):
-            rows = slice(part * HALF, (part + 1) * HALF)
-            slab = high_ref[rows, cut].astype(F32) + low_ref[rows, cut].astype(F32)
-            inner_ref[rows, put] = slab - mm(cols_ref[rows, :], stack(band))
+    solve = left_pair(solve)
+    for place in range(0, inner_ref.shape[1], chunk):
+        cut = slice(begin + place, begin + place + chunk)
+        for rows, inner in local_part(cut, high_ref, low_ref, sums_ref, cols_ref, solve):
+            inner_ref[rows, place : place + chunk] = inner
 
 
 def inside_kernel(chunk, inputs, *refs):
@@ -281,60 +305,71 @@
     subtract_inside(chunk, 0, high_ref, low_ref, sums_ref, cols_ref, solve, inner_ref)
 
 
-def inside_more_kernel(chunk, high_ref, low_ref, sums_ref, solve_ref, cols_ref, inner_ref):
-    begin = high_ref.shape[1] - inner_ref.shape[1]
-    subtract_inside(chunk, begin, high_ref, low_ref, sums_ref, cols_ref, solve_ref[...], inner_ref)
-
-
-def finish_kernel(chunk, *refs):
-    across_refs, beside_refs, refs = refs[:2], refs[2:5], refs[5:]
-    down_ref, up_ref, ends_ref = refs[:3]
-    inner_refs, (out_ref, obuf, coeff_ref, sems) = refs[3:5], refs[5:]
-    columns = 2 * inner_refs[0].shape[1]
+def from_neighbours(across, beside):
     row, count = lax.axis_index("row"), lax.axis_size("row")
     is_even = lax.rem(row, 2) == 0
-
-    def messages(cut):
-        across = jnp.concatenate([ref[:, cut] for ref in across_refs], axis=0)
-        across = jnp.where((row > 0) & (row < count - 1), across, 0.0)
-        first, left, right = beside_refs
-        middle = left.shape[1]
-        if cut.start < middle:
-            last = left[:, cut]
-        else:
-            last = right[:, cut.start - middle : cut.stop - middle]
-        beside = jnp.concatenate([first[:, cut], last], axis=0)
-        below = jnp.where(is_even, beside, across)
-        above = jnp.where(is_even, across, beside)
-        return down_ref[:, cut], up_ref[:, cut], below, above
-
-    own_side, own_top, next_side, prev_top = messages(slice(columns, columns + EXTRA))
-    _, n7, c7 = straddling(own_top + next_side, 0)
-    tau1, n1, c1 = straddling(prev_top + own_side, SWEEPS)
+    across = jnp.where((row > 0) & (row < count - 1), across, 0.0)
+    return jnp.where(is_even, beside, across), jnp.where(is_even, across, beside)
+
+
+def inside_more_kernel(chunk, begin, *refs):
+    high_ref, low_ref, sums_ref, solve_ref, cols_ref = refs[:5]
+    across_ref, beside_ref, down_ref, up_ref, ends_ref, inner_ref, effect_ref = refs[5:]
+    extra = slice(down_ref.shape[1] - EXTRA, down_ref.shape[1])
+
+    def unfold(a):
+        return jnp.concatenate([a, pltpu.roll(a, 128 - 2 * SWEEPS, 1)], axis=0)
+
+    below, above = from_neighbours(across_ref[:, extra], beside_ref[:, extra])
+    own_side = down_ref[:, extra]
+    _, n7, c7 = straddling(up_ref[:, extra] + unfold(below), 0)
+    tau1, n1, c1 = straddling(unfold(above) + own_side, SWEEPS)
     e1 = own_side * tau1
     for s in range(SWEEPS - 1):
         row7, row1 = c7[s : s + 1], c1[s : s + 1]
         c7 = eliminate(c7, n7[:, s : s + 1], row7, s)
         c1 = eliminate(c1, n1[:, s : s + 1], row1, s)
         c1 = eliminate(c1, -e1[:, SWEEPS + s : SWEEPS + s + 1], row7, s)
-    join = split(jnp.concatenate([c1, c7], axis=0)[:, : 2 * SWEEPS])
-    effect = ends_ref[:, : 6 * SWEEPS]
-
+    join = jnp.concatenate([c1, c7], axis=0)
+    join = join + pltpu.roll(join, 2 * SWEEPS, 1) + pltpu.roll(join, 4 * SWEEPS, 1)
+    high, low = split(mm(ends_ref[:, : 6 * SWEEPS], stack(join)))
+    group = iota(high.shape, 1) // (2 * SWEEPS)
+    effect = jnp.where(group == 1, low.astype(F32), high.astype(F32))
+    effect_ref[...] = effect.astype(BF16)
+    subtract_inside(chunk, begin, high_ref, low_ref, sums_ref, cols_ref, solve_ref[...], inner_ref)
+
+
+def finish_kernel(chunk, *refs):
+    first_across, last_across, first_beside, last_beside = refs[:4]
+    down_ref, up_ref, effect_ref, high_ref, low_ref, sums_ref, cols_ref, solve_ref = refs[4:12]
+    inner_refs, (out_ref, obuf, sems) = refs[12:14], refs[14:]
+    columns = high_ref.shape[1]
+    effect = effect_ref[:, : 6 * SWEEPS]
+    solve = left_pair(solve_ref[...])
+
+    def messages(cut):
+        across = jnp.concatenate([first_across[:, cut], last_across[:, cut]], axis=0)
+        beside = jnp.concatenate([first_beside[:, cut], last_beside[:, cut]], axis=0)
+        below, above = from_neighbours(across, beside)
+        return stack(jnp.concatenate([up_ref[:, cut] + below, down_ref[:, cut] + above], axis=0))
+
+    stores = []
+    pieces = []
+    for ref in inner_refs:
+        for place in range(0, ref.shape[1], chunk):
+            pieces.append((ref, place))
     for j in range(columns // chunk):
         cut = slice(j * chunk, (j + 1) * chunk)
-        down, up, below, above = messages(cut)
-        incoming = jnp.concatenate([up + below, down + above], axis=0)
-        coeff_ref[:, cut] = stack(mm3(join, split(incoming)))
-
-    stores = []
-    for j in range(columns // chunk):
-        cut = slice(j * chunk, (j + 1) * chunk)
-        part, place = divmod(j * chunk, columns // 2)
-        inner = inner_refs[part][:, place : place + chunk]
-        obuf[:, cut] = inner - mm(effect, coeff_ref[:, cut])
+        coeff = messages(cut)
+        if j < len(pieces):
+            ref, place = pieces[j]
+            obuf[:, cut] = ref[:, place : place + chunk] - mm(effect, coeff)
+        else:
+            for rows, inner in local_part(cut, high_ref, low_ref, sums_ref, cols_ref, solve):
+                obuf[rows, cut] = inner - mm(effect[rows], coeff)
         cut = pl.ds(j * chunk, chunk)
         stores.append(pltpu.make_async_copy(obuf.at[:, cut], out_ref.at[:, cut], sems.at[j]))
-        stores[-1].start(priority=j % 2)
+        stores[-1].start()
     for store in stores:
         store.wait()
 
@@ -431,10 +466,11 @@
     )(down, up, got_beside)
     got_late = lax.ppermute(late, ("row", "col"), over_chips)
 
-    half = shape((rows, columns // 2), F32)
+    inside_first = (chunks + 1) // 2 * chunk
+    inside_next = (chunks + 2) // 4 * chunk
     inner, ends, cols = pl.pallas_call(
         functools.partial(inside_kernel, chunk, len(vectors)),
-        out_shape=(half, shape((rows, 128), BF16), shape((rows, 3 * BAND), BF16)),
+        out_shape=(shape((rows, inside_first), F32), shape((rows, 128), BF16), shape((rows, 3 * BAND), BF16)),
         in_specs=[vmem] * (len(vectors) + 6),
         out_specs=(vmem,) * 3,
         compiler_params=params,
@@ -444,38 +480,37 @@
 
     latest = pl.pallas_call(
         functools.partial(complete_kernel, 1),
-        out_shape=(shape((8, columns // 2), F32), shape((8, columns // 2 + EXTRA), F32)),
+        out_shape=shape((8, columns), F32),
         in_specs=[vmem] * 4,
-        out_specs=(vmem,) * 2,
+        out_specs=vmem,
         compiler_params=params,
         name="complete_odd",
     )(down, up, got_across, ends)
-    got_latest = [lax.ppermute(part, "row", on_chip) for part in latest]
-
-    more = pl.pallas_call(
-        functools.partial(inside_more_kernel, chunk),
-        out_shape=half,
-        in_specs=[vmem] * 5,
-        out_specs=vmem,
+    got_latest = lax.ppermute(latest, "row", on_chip)
+
+    more, effect = pl.pallas_call(
+        functools.partial(inside_more_kernel, chunk, inside_first),
+        out_shape=(shape((rows, inside_next), F32), shape((rows, 128), BF16)),
+        in_specs=[vmem] * 10,
+        out_specs=(vmem,) * 2,
         compiler_params=params,
         cost_estimate=cost(2, rows * columns * 240),
         name="inside_more",
-    )(high, low, sums, solve, cols)
+    )(high, low, sums, solve, cols, got_across, got_beside, down, up, ends)
 
     return pl.pallas_call(
         functools.partial(finish_kernel, chunk),
         out_shape=shape((rows, columns), F32),
-        in_specs=[vmem] * 10,
+        in_specs=[vmem] * 14,
         out_specs=hbm,
         scratch_shapes=[
             pltpu.VMEM((rows, columns), F32),
-            pltpu.VMEM((6 * SWEEPS, columns), BF16),
             pltpu.SemaphoreType.DMA((chunks,)),
         ],
         compiler_params=params,
         cost_estimate=cost(2, rows * columns * 200),
         name="finish",
-    )(got_across, got_late, got_beside, *got_latest, down, up, ends, inner, more)
+    )(got_across, got_late, got_beside, got_latest, down, up, effect, high, low, sums, cols, solve, inner, more)
 
 
 def solution(mesh):

time: 16.2 us -> 15.5 us (0.957)
  Pallas kernels: 9.47 us -> 9 us
  starting transfers between devices: 6.5 us -> 6.08 us
    pallas_call x1, Pallas kernels: 2.8 us -> 2.36 us  [local(): pl.pallas_call(functools.partial(finish_kernel, chunk), out_shape=shape((...]
    ppermute x2 -> x1, starting transfers between devices: 0.58 us -> 0.15 us  [local(): got_latest = lax.ppermute(latest, 'row', on_chip)]
  transfers between devices with their start and end apart: 6 -> 5, of which waited for: 0 -> 2; matrix products, arithmetic and copies ran while one was open for 0% -> 0% of each run, Pallas kernels for 34% -> 35%
where the time goes in v2:
time: 15.5 us; the launch traced here: 15.3 us
  Pallas kernels  9 us (58%)
  starting transfers between devices  6.08 us (39%)
  waiting for transfers between devices  0.17 us (1%)
    ppermute x1, starting transfers between devices, local(): vectors = (reflectors, lax.ppermute(reflectors, 'col', [(0, 1), (1, 0)]))  2.97 us
    pallas_call x1, Pallas kernels, local(): pl.pallas_call(functools.partial(finish_kernel, chunk), out_shape=shape((...  2.36 us
    pallas_call x1, Pallas kernels, local(): pl.pallas_call(prepare_kernel, out_shape=(shape((rows, columns), BF16), s...  2.32 us
    ppermute x1, starting transfers between devices, local(): got_across = lax.ppermute(across, ('row', 'col'), over_chips)  1.67 us
    pallas_call x1, Pallas kernels, local(): pl.pallas_call(functools.partial(inside_kernel, chunk, len(vectors)), out...  1.39 us
    ppermute x1, starting transfers between devices, local(): got_late = lax.ppermute(late, ('row', 'col'), over_chips)  1.24 us
    pallas_call x1, Pallas kernels, local(): pl.pallas_call(functools.partial(project_kernel, chunk, len(vectors)), ou...  1.22 us
    pallas_call x1, Pallas kernels, local(): pl.pallas_call(functools.partial(inside_more_kernel, chunk, inside_first)...  1.09 us
  transfers between devices with their start and end apart: 5, of which 2 were waited for; matrix products, arithmetic and copies ran while one was open for 0% of the time, Pallas kernels for 35%

profile of v2, /device:TPU:0, one launch (start us, length us, event | category | flops | bytes accessed | tf_op | source)
XLA Modules:
  0.0 15.3 jit_solution(13718364067437639035)
XLA Ops:
  0.0 0.0 copy-start
  0.0 3.0 %collective-permute-start = (f32[8,512]{1,0:T(8,128)}, f32[8,512]{1,0:T(8,128)S(1)}, u32[]{:S(2)}, u32[]{:S(2)}) collective-permute-start(f32[8,512]{1,0:T(8,128)} %refs_0_.3), channel_id=1, source_target_pairs={{0,1},{1,0},{2,3},{3,2},{4,5},{5,4},{6,7},{7,6},{8,9},{9,8},{10,11... | collective-permute-start | bytes 49160 | tf_op jit(solution)/shard_map/ppermute | solution.py:398
  3.0 2.3 %prepare.1 = (bf16[512,2048]{1,0:T(8,128)(2,1)S(1)}, bf16[512,2048]{1,0:T(8,128)(2,1)S(1)}, s32[16,512]{1,0:T(8,128)S(1)}) custom-call(f32[512,2048]{1,0:T(8,128)} %x_ref.1, s32[16]{0:T(128)} %off_ref.1), custom_call_target="tpu_custom_call" | custom-call | bytes 8388608 | tf_op jit(solution)/shard_map/prepare/pallas_call | solution.py:404
  5.3 0.0 collective-permute-done.refs_1_
  5.3 0.0 copy-done
  5.3 1.2 %project.1 = (f32[112,2048]{1,0:T(8,128)S(1)}, f32[8,2176]{1,0:T(8,128)S(1)}, f32[8,2176]{1,0:T(8,128)S(1)}, f32[16,2176]{1,0:T(8,128)S(1)}, f32[16,2176]{1,0:T(8,128)S(1)}, /*index=5*/f32[112,128]{1,0:T(8,128)S(1)}) custom-call(f32[8,512]{1,0:T(8,128)S(1)} %copy-done, f32[8,512]{1,0:T(8,128)S(1)} %collective-permute-done.refs_1_, ...), custom_call_target="tpu_custom_call" | custom-call | flops 251658240 | bytes 8388608 | tf_op jit(solution)/shard_map/project/pallas_call | solution.py:426
  6.5 0.1 collective-permute-start.2
  6.6 1.7 %collective-permute-start.1 = (f32[8,2176]{1,0:T(8,128)S(1)}, f32[8,2176]{1,0:T(8,128)S(1)}, u32[]{:S(2)}, u32[]{:S(2)}) collective-permute-start(f32[8,2176]{1,0:T(8,128)S(1)} %get-tuple-element.22), channel_id=1, source_target_pairs={{2,4},{3,5},{6,8},{7,9},{10,12},{11,13},{14,16},{15,17},{18,20},{1... | collective-permute-start | bytes 208904 | tf_op jit(solution)/shard_map/ppermute | solution.py:458
  8.3 0.0 collective-permute-done.2.got_ref.refs_6_.refs_2_
  8.3 0.3 %complete_even.1.refs_7_ = f32[8,2176]{1,0:T(8,128)S(1)} custom-call(f32[16,2176]{1,0:T(8,128)S(1)} %get-tuple-element.23.down_ref.refs_7_.refs_4_, f32[16,2176]{1,0:T(8,128)S(1)} %get-tuple-element.24.up_ref.refs_8_.refs_5_, f32[8,2176]{1,0:T(8,128)S(1)} %collective-permute-done.2.got_ref.refs_6_.refs_2_), custom_call_target="tpu_custom_call" | custom-call | tf_op jit(solution)/shard_map/complete_even/pallas_call | solution.py:459
  8.6 1.2 %collective-permute-start.3 = (f32[8,2176]{1,0:T(8,128)S(1)}, f32[8,2176]{1,0:T(8,128)S(1)}, u32[]{:S(2)}, u32[]{:S(2)}) collective-permute-start(f32[8,2176]{1,0:T(8,128)S(1)} %complete_even.1.refs_7_), channel_id=1, source_target_pairs={{2,4},{3,5},{6,8},{7,9},{10,12},{11,13},{14,16},{15,17},{18,20},{1... | collective-permute-start | bytes 208904 | tf_op jit(solution)/shard_map/ppermute | solution.py:467
  9.8 1.4 %inside.1 = (f32[512,1024]{1,0:T(8,128)S(1)}, bf16[512,128]{1,0:T(8,128)(2,1)S(1)}, bf16[512,240]{1,0:T(8,128)(2,1)S(1)}) custom-call(f32[8,512]{1,0:T(8,128)S(1)} %copy-done, f32[8,512]{1,0:T(8,128)S(1)} %collective-permute-done.refs_1_, s32[16,512]{1,0:T(8,128)S(1)} %get-tuple-element.19.refs_2_, ...), custom_call_target="tpu_custom_call" | custom-call | flops 251658240 | bytes 8388608 | tf_op jit(solution)/shard_map/inside/pallas_call | solution.py:471
  11.2 0.0 collective-permute-done.1.got_ref.refs_5_.refs_0_
  11.2 0.3 %complete_odd.1 = f32[8,2048]{1,0:T(8,128)S(1)} custom-call(f32[16,2176]{1,0:T(8,128)S(1)} %get-tuple-element.23.down_ref.refs_7_.refs_4_, f32[16,2176]{1,0:T(8,128)S(1)} %get-tuple-element.24.up_ref.refs_8_.refs_5_, f32[8,2176]{1,0:T(8,128)S(1)} %collective-permute-done.1.got_ref.refs_5_.refs_0_, bf16[512,128]{1,0:T(8,128)(2,1)S(1)} %get-tuple-element.28.refs_0_.refs_9_), custom_call_target="tpu_custom_call" | custom-call | tf_op jit(solution)/shard_map/complete_odd/pallas_call | solution.py:481
  11.6 0.1 collective-permute-start.4
  11.7 1.1 %inside_more.1 = (f32[512,512]{1,0:T(8,128)S(1)}, bf16[512,128]{1,0:T(8,128)(2,1)S(1)}) custom-call(bf16[512,2048]{1,0:T(8,128)(2,1)S(1)} %get-tuple-element.20.refs_3_.refs_0_.refs_7_, bf16[512,2048]{1,0:T(8,128)(2,1)S(1)} %get-tuple-element.21.refs_4_.refs_1_.refs_8_, f32[112,2048]{1,0:T(8,128)S(1)} %get-tuple-element.26.refs_5_.refs_2_.refs_9_, ...), custom_call_target="tpu_custom_call" | custom-call | flops 251658240 | bytes 8388608 | tf_op jit(solution)/shard_map/inside_more/pallas_call | solution.py:491
  12.8 0.1 collective-permute-done.4.refs_3_
  12.9 0.1 collective-permute-done.3.refs_1_
  13.0 2.4 %finish.1 = f32[512,2048]{1,0:T(8,128)} custom-call(f32[8,2176]{1,0:T(8,128)S(1)} %collective-permute-done.1.got_ref.refs_5_.refs_0_, f32[8,2176]{1,0:T(8,128)S(1)} %collective-permute-done.3.refs_1_, f32[8,2176]{1,0:T(8,128)S(1)} %collective-permute-done.2.got_ref.refs_6_.refs_2_, f32[8,2048]{1,0:T(8,128)S(1)} %collective-permute-done.4.refs_3_, ...), custom_call_target="tpu_custom_call" | custom-call | flops 209715200 | bytes 8388608 | tf_op jit(solution)/shard_map/finish/pallas_call | solution.py:501
Async XLA Ops:
  0.0 5.3 %copy-start = (f32[8,512]{1,0:T(8,128)S(1)}, f32[8,512]{1,0:T(8,128)}, u32[]{:S(2)}) copy-start(f32[8,512]{1,0:T(8,128)} %refs_0_.3) | copy-start | bytes 49156
  0.0 5.3 %collective-permute-start = (f32[8,512]{1,0:T(8,128)}, f32[8,512]{1,0:T(8,128)S(1)}, u32[]{:S(2)}, u32[]{:S(2)}) collective-permute-start(f32[8,512]{1,0:T(8,128)} %refs_0_.3), channel_id=1, source_target_pairs={{0,1},{1,0},{2,3},{3,2},{4,5},{5,4},{6,7},{7,6},{8,9},{9,8},{10,11... | collective-permute-start | bytes 49160 | tf_op jit(solution)/shard_map/ppermute | solution.py:398
  6.5 1.7 %collective-permute-start.2 = (f32[8,2176]{1,0:T(8,128)S(1)}, f32[8,2176]{1,0:T(8,128)S(1)}, u32[]{:S(2)}, u32[]{:S(2)}) collective-permute-start(f32[8,2176]{1,0:T(8,128)S(1)} %get-tuple-element.25), channel_id=1, source_target_pairs={{0,2},{4,6},{8,10},{12,14},{16,18},{20,22},{24,26},{28,30},{2,0},{... | collective-permute-start | bytes 208904 | tf_op jit(solution)/shard_map/ppermute | solution.py:457
  6.6 4.6 %collective-permute-start.1 = (f32[8,2176]{1,0:T(8,128)S(1)}, f32[8,2176]{1,0:T(8,128)S(1)}, u32[]{:S(2)}, u32[]{:S(2)}) collective-permute-start(f32[8,2176]{1,0:T(8,128)S(1)} %get-tuple-element.22), channel_id=1, source_target_pairs={{2,4},{3,5},{6,8},{7,9},{10,12},{11,13},{14,16},{15,17},{18,20},{1... | collective-permute-start | bytes 208904 | tf_op jit(solution)/shard_map/ppermute | solution.py:458
  8.6 4.4 %collective-permute-start.3 = (f32[8,2176]{1,0:T(8,128)S(1)}, f32[8,2176]{1,0:T(8,128)S(1)}, u32[]{:S(2)}, u32[]{:S(2)}) collective-permute-start(f32[8,2176]{1,0:T(8,128)S(1)} %complete_even.1.refs_7_), channel_id=1, source_target_pairs={{2,4},{3,5},{6,8},{7,9},{10,12},{11,13},{14,16},{15,17},{18,20},{1... | collective-permute-start | bytes 208904 | tf_op jit(solution)/shard_map/ppermute | solution.py:467
  11.6 1.3 %collective-permute-start.4 = (f32[8,2048]{1,0:T(8,128)S(1)}, f32[8,2048]{1,0:T(8,128)S(1)}, u32[]{:S(2)}, u32[]{:S(2)}) collective-permute-start(f32[8,2048]{1,0:T(8,128)S(1)} %complete_odd.1), channel_id=1, source_target_pairs={{0,2},{4,6},{8,10},{12,14},{16,18},{20,22},{24,26},{28,30},{2,0},{... | collective-permute-start | bytes 196616 | tf_op jit(solution)/shard_map/ppermute | solution.py:489

commit v3 on v2

--- a/solution.py
+++ b/solution.py
@@ -383,6 +383,7 @@
     assert rows == ROWS and columns % 256 == 0
     chunk = 256 if columns % 512 == 0 else 128
     chunks = columns // chunk
+    wide = 2 * chunk if chunks % 8 == 0 else chunk
     count = lax.axis_size("row")
     groups = lax.axis_size("col")
     vmem = pl.BlockSpec(memory_space=pltpu.VMEM)
@@ -424,7 +425,7 @@
     own = shape((SWEEPS, columns + EXTRA), F32)
     eight = shape((8, columns + EXTRA), F32)
     sums, beside, across, down, up, solve = pl.pallas_call(
-        functools.partial(project_kernel, chunk, len(vectors)),
+        functools.partial(project_kernel, wide, len(vectors)),
         out_shape=(
             shape((LOCAL, columns), F32),
             eight,
@@ -466,10 +467,10 @@
     )(down, up, got_beside)
     got_late = lax.ppermute(late, ("row", "col"), over_chips)
 
-    inside_first = (chunks + 1) // 2 * chunk
     inside_next = (chunks + 2) // 4 * chunk
+    inside_first = columns - inside_next
     inner, ends, cols = pl.pallas_call(
-        functools.partial(inside_kernel, chunk, len(vectors)),
+        functools.partial(inside_kernel, wide, len(vectors)),
         out_shape=(shape((rows, inside_first), F32), shape((rows, 128), BF16), shape((rows, 3 * BAND), BF16)),
         in_specs=[vmem] * (len(vectors) + 6),
         out_specs=(vmem,) * 3,
@@ -489,7 +490,7 @@
     got_latest = lax.ppermute(latest, "row", on_chip)
 
     more, effect = pl.pallas_call(
-        functools.partial(inside_more_kernel, chunk, inside_first),
+        functools.partial(inside_more_kernel, wide, inside_first),
         out_shape=(shape((rows, inside_next), F32), shape((rows, 128), BF16)),
         in_specs=[vmem] * 10,
         out_specs=(vmem,) * 2,

time: 15.5 us -> 15.5 us (level)
  Pallas kernels: 9 us -> 8.82 us
  waiting for transfers between devices: 0.17 us -> 0.34 us
    pallas_call x3, Pallas kernels: 3.69 us -> 3.51 us  [the longest x1 1.39 us: local(): pl.pallas_call(functools.partial(inside_kernel, wide, len(vectors)), out_...]
    ppermute x1, waiting for transfers between devices: 0.08 us -> 0.25 us  [local(): got_latest = lax.ppermute(latest, 'row', on_chip)]
  transfers between devices with their start and end apart: 5 -> 5, of which waited for: 2 -> 2; matrix products, arithmetic and copies ran while one was open for 0% -> 0% of each run, Pallas kernels for 35% -> 34%
where the time goes in v3:
time: 15.5 us; the launch traced here: 15.3 us
  Pallas kernels  8.82 us (57%)
  starting transfers between devices  6.1 us (39%)
  waiting for transfers between devices  0.34 us (2%)
    ppermute x1, starting transfers between devices, local(): vectors = (reflectors, lax.ppermute(reflectors, 'col', [(0, 1), (1, 0)]))  2.97 us
    pallas_call x1, Pallas kernels, local(): pl.pallas_call(functools.partial(finish_kernel, chunk), out_shape=shape((...  2.37 us
    pallas_call x1, Pallas kernels, local(): pl.pallas_call(prepare_kernel, out_shape=(shape((rows, columns), BF16), s...  2.32 us
    ppermute x1, starting transfers between devices, local(): got_across = lax.ppermute(across, ('row', 'col'), over_chips)  1.67 us
    pallas_call x1, Pallas kernels, local(): pl.pallas_call(functools.partial(inside_kernel, wide, len(vectors)), out_...  1.39 us
    ppermute x1, starting transfers between devices, local(): got_late = lax.ppermute(late, ('row', 'col'), over_chips)  1.24 us
    pallas_call x1, Pallas kernels, local(): pl.pallas_call(functools.partial(project_kernel, wide, len(vectors)), out...  1.22 us
    pallas_call x1, Pallas kernels, local(): pl.pallas_call(functools.partial(inside_more_kernel, wide, inside_first),...  0.9 us
  transfers between devices with their start and end apart: 5, of which 2 were waited for; matrix products, arithmetic and copies ran while one was open for 0% of the time, Pallas kernels for 34%

profile of v3, /device:TPU:0, one launch (start us, length us, event | category | flops | bytes accessed | tf_op | source)
XLA Modules:
  0.0 15.3 jit_solution(5957471588617466521)
XLA Ops:
  0.0 0.0 copy-start
  0.0 3.0 %collective-permute-start = (f32[8,512]{1,0:T(8,128)}, f32[8,512]{1,0:T(8,128)S(1)}, u32[]{:S(2)}, u32[]{:S(2)}) collective-permute-start(f32[8,512]{1,0:T(8,128)} %refs_0_.3), channel_id=1, source_target_pairs={{0,1},{1,0},{2,3},{3,2},{4,5},{5,4},{6,7},{7,6},{8,9},{9,8},{10,11... | collective-permute-start | bytes 49160 | tf_op jit(solution)/shard_map/ppermute | solution.py:399
  3.0 2.3 %prepare.1 = (bf16[512,2048]{1,0:T(8,128)(2,1)S(1)}, bf16[512,2048]{1,0:T(8,128)(2,1)S(1)}, s32[16,512]{1,0:T(8,128)S(1)}) custom-call(f32[512,2048]{1,0:T(8,128)} %x_ref.1, s32[16]{0:T(128)} %off_ref.1), custom_call_target="tpu_custom_call" | custom-call | bytes 8388608 | tf_op jit(solution)/shard_map/prepare/pallas_call | solution.py:405
  5.3 0.0 collective-permute-done.refs_1_
  5.3 0.0 copy-done
  5.3 1.2 %project.1 = (f32[112,2048]{1,0:T(8,128)S(1)}, f32[8,2176]{1,0:T(8,128)S(1)}, f32[8,2176]{1,0:T(8,128)S(1)}, f32[16,2176]{1,0:T(8,128)S(1)}, f32[16,2176]{1,0:T(8,128)S(1)}, /*index=5*/f32[112,128]{1,0:T(8,128)S(1)}) custom-call(f32[8,512]{1,0:T(8,128)S(1)} %copy-done, f32[8,512]{1,0:T(8,128)S(1)} %collective-permute-done.refs_1_, ...), custom_call_target="tpu_custom_call" | custom-call | flops 251658240 | bytes 8388608 | tf_op jit(solution)/shard_map/project/pallas_call | solution.py:427
  6.5 0.1 collective-permute-start.2
  6.6 1.7 %collective-permute-start.1 = (f32[8,2176]{1,0:T(8,128)S(1)}, f32[8,2176]{1,0:T(8,128)S(1)}, u32[]{:S(2)}, u32[]{:S(2)}) collective-permute-start(f32[8,2176]{1,0:T(8,128)S(1)} %get-tuple-element.22), channel_id=1, source_target_pairs={{2,4},{3,5},{6,8},{7,9},{10,12},{11,13},{14,16},{15,17},{18,20},{1... | collective-permute-start | bytes 208904 | tf_op jit(solution)/shard_map/ppermute | solution.py:459
  8.3 0.0 collective-permute-done.2.got_ref.refs_6_.refs_2_
  8.3 0.3 %complete_even.1.refs_7_ = f32[8,2176]{1,0:T(8,128)S(1)} custom-call(f32[16,2176]{1,0:T(8,128)S(1)} %get-tuple-element.23.down_ref.refs_7_.refs_4_, f32[16,2176]{1,0:T(8,128)S(1)} %get-tuple-element.24.up_ref.refs_8_.refs_5_, f32[8,2176]{1,0:T(8,128)S(1)} %collective-permute-done.2.got_ref.refs_6_.refs_2_), custom_call_target="tpu_custom_call" | custom-call | tf_op jit(solution)/shard_map/complete_even/pallas_call | solution.py:460
  8.6 1.2 %collective-permute-start.3 = (f32[8,2176]{1,0:T(8,128)S(1)}, f32[8,2176]{1,0:T(8,128)S(1)}, u32[]{:S(2)}, u32[]{:S(2)}) collective-permute-start(f32[8,2176]{1,0:T(8,128)S(1)} %complete_even.1.refs_7_), channel_id=1, source_target_pairs={{2,4},{3,5},{6,8},{7,9},{10,12},{11,13},{14,16},{15,17},{18,20},{1... | collective-permute-start | bytes 208904 | tf_op jit(solution)/shard_map/ppermute | solution.py:468
  9.8 1.4 %inside.1 = (f32[512,1536]{1,0:T(8,128)S(1)}, bf16[512,128]{1,0:T(8,128)(2,1)S(1)}, bf16[512,240]{1,0:T(8,128)(2,1)S(1)}) custom-call(f32[8,512]{1,0:T(8,128)S(1)} %copy-done, f32[8,512]{1,0:T(8,128)S(1)} %collective-permute-done.refs_1_, s32[16,512]{1,0:T(8,128)S(1)} %get-tuple-element.19.refs_2_, ...), custom_call_target="tpu_custom_call" | custom-call | flops 251658240 | bytes 8388608 | tf_op jit(solution)/shard_map/inside/pallas_call | solution.py:472
  11.2 0.0 collective-permute-done.1.got_ref.refs_5_.refs_0_
  11.2 0.3 %complete_odd.1 = f32[8,2048]{1,0:T(8,128)S(1)} custom-call(f32[16,2176]{1,0:T(8,128)S(1)} %get-tuple-element.23.down_ref.refs_7_.refs_4_, f32[16,2176]{1,0:T(8,128)S(1)} %get-tuple-element.24.up_ref.refs_8_.refs_5_, f32[8,2176]{1,0:T(8,128)S(1)} %collective-permute-done.1.got_ref.refs_5_.refs_0_, bf16[512,128]{1,0:T(8,128)(2,1)S(1)} %get-tuple-element.28.refs_0_.refs_9_), custom_call_target="tpu_custom_call" | custom-call | tf_op jit(solution)/shard_map/complete_odd/pallas_call | solution.py:482
  11.6 0.2 %collective-permute-start.4 = (f32[8,2048]{1,0:T(8,128)S(1)}, f32[8,2048]{1,0:T(8,128)S(1)}, u32[]{:S(2)}, u32[]{:S(2)}) collective-permute-start(f32[8,2048]{1,0:T(8,128)S(1)} %complete_odd.1), channel_id=1, source_target_pairs={{0,2},{4,6},{8,10},{12,14},{16,18},{20,22},{24,26},{28,30},{2,0},{... | collective-permute-start | bytes 196616 | tf_op jit(solution)/shard_map/ppermute | solution.py:490
  11.7 0.9 %inside_more.1 = (f32[512,512]{1,0:T(8,128)S(1)}, bf16[512,128]{1,0:T(8,128)(2,1)S(1)}) custom-call(bf16[512,2048]{1,0:T(8,128)(2,1)S(1)} %get-tuple-element.20.refs_3_.refs_0_.refs_7_, bf16[512,2048]{1,0:T(8,128)(2,1)S(1)} %get-tuple-element.21.refs_4_.refs_1_.refs_8_, f32[112,2048]{1,0:T(8,128)S(1)} %get-tuple-element.26.refs_5_.refs_2_.refs_9_, ...), custom_call_target="tpu_custom_call" | custom-call | flops 251658240 | bytes 8388608 | tf_op jit(solution)/shard_map/inside_more/pallas_call | solution.py:492
  12.6 0.3 %collective-permute-done.4.refs_3_ = f32[8,2048]{1,0:T(8,128)S(1)} collective-permute-done((f32[8,2048]{1,0:T(8,128)S(1)}, f32[8,2048]{1,0:T(8,128)S(1)}, u32[]{:S(2)}, u32[]{:S(2)}) %collective-permute-start.4) | collective-permute-done | bytes 65568 | tf_op jit(solution)/shard_map/ppermute | solution.py:490
  12.9 0.1 collective-permute-done.3.refs_1_
  13.0 2.4 %finish.1 = f32[512,2048]{1,0:T(8,128)} custom-call(f32[8,2176]{1,0:T(8,128)S(1)} %collective-permute-done.1.got_ref.refs_5_.refs_0_, f32[8,2176]{1,0:T(8,128)S(1)} %collective-permute-done.3.refs_1_, f32[8,2176]{1,0:T(8,128)S(1)} %collective-permute-done.2.got_ref.refs_6_.refs_2_, f32[8,2048]{1,0:T(8,128)S(1)} %collective-permute-done.4.refs_3_, ...), custom_call_target="tpu_custom_call" | custom-call | flops 209715200 | bytes 8388608 | tf_op jit(solution)/shard_map/finish/pallas_call | solution.py:502
Async XLA Ops:
  0.0 5.3 %copy-start = (f32[8,512]{1,0:T(8,128)S(1)}, f32[8,512]{1,0:T(8,128)}, u32[]{:S(2)}) copy-start(f32[8,512]{1,0:T(8,128)} %refs_0_.3) | copy-start | bytes 49156
  0.0 5.3 %collective-permute-start = (f32[8,512]{1,0:T(8,128)}, f32[8,512]{1,0:T(8,128)S(1)}, u32[]{:S(2)}, u32[]{:S(2)}) collective-permute-start(f32[8,512]{1,0:T(8,128)} %refs_0_.3), channel_id=1, source_target_pairs={{0,1},{1,0},{2,3},{3,2},{4,5},{5,4},{6,7},{7,6},{8,9},{9,8},{10,11... | collective-permute-start | bytes 49160 | tf_op jit(solution)/shard_map/ppermute | solution.py:399
  6.5 1.7 %collective-permute-start.2 = (f32[8,2176]{1,0:T(8,128)S(1)}, f32[8,2176]{1,0:T(8,128)S(1)}, u32[]{:S(2)}, u32[]{:S(2)}) collective-permute-start(f32[8,2176]{1,0:T(8,128)S(1)} %get-tuple-element.25), channel_id=1, source_target_pairs={{0,2},{4,6},{8,10},{12,14},{16,18},{20,22},{24,26},{28,30},{2,0},{... | collective-permute-start | bytes 208904 | tf_op jit(solution)/shard_map/ppermute | solution.py:458
  6.6 4.6 %collective-permute-start.1 = (f32[8,2176]{1,0:T(8,128)S(1)}, f32[8,2176]{1,0:T(8,128)S(1)}, u32[]{:S(2)}, u32[]{:S(2)}) collective-permute-start(f32[8,2176]{1,0:T(8,128)S(1)} %get-tuple-element.22), channel_id=1, source_target_pairs={{2,4},{3,5},{6,8},{7,9},{10,12},{11,13},{14,16},{15,17},{18,20},{1... | collective-permute-start | bytes 208904 | tf_op jit(solution)/shard_map/ppermute | solution.py:459
  8.6 4.4 %collective-permute-start.3 = (f32[8,2176]{1,0:T(8,128)S(1)}, f32[8,2176]{1,0:T(8,128)S(1)}, u32[]{:S(2)}, u32[]{:S(2)}) collective-permute-start(f32[8,2176]{1,0:T(8,128)S(1)} %complete_even.1.refs_7_), channel_id=1, source_target_pairs={{2,4},{3,5},{6,8},{7,9},{10,12},{11,13},{14,16},{15,17},{18,20},{1... | collective-permute-start | bytes 208904 | tf_op jit(solution)/shard_map/ppermute | solution.py:468
  11.6 1.3 %collective-permute-start.4 = (f32[8,2048]{1,0:T(8,128)S(1)}, f32[8,2048]{1,0:T(8,128)S(1)}, u32[]{:S(2)}, u32[]{:S(2)}) collective-permute-start(f32[8,2048]{1,0:T(8,128)S(1)} %complete_odd.1), channel_id=1, source_target_pairs={{0,2},{4,6},{8,10},{12,14},{16,18},{20,22},{24,26},{28,30},{2,0},{... | collective-permute-start | bytes 196616 | tf_op jit(solution)/shard_map/ppermute | solution.py:490

commit v4 on v2

--- a/solution.py
+++ b/solution.py
@@ -353,21 +353,33 @@
         below, above = from_neighbours(across, beside)
         return stack(jnp.concatenate([up_ref[:, cut] + below, down_ref[:, cut] + above], axis=0))
 
-    stores = []
-    pieces = []
+    cuts = []
+    start = 0
     for ref in inner_refs:
         for place in range(0, ref.shape[1], chunk):
-            pieces.append((ref, place))
-    for j in range(columns // chunk):
-        cut = slice(j * chunk, (j + 1) * chunk)
+            cuts.append((start + place, chunk, ref, place))
+        start += ref.shape[1]
+
+    def halved(cut):
+        begin, width, ref, place = cut
+        width //= 2
+        return [(begin, width, ref, place), (begin + width, width, ref, place + width)]
+
+    if chunk == 256:
+        cuts = halved(cuts[0]) + cuts[1:-1] + halved(cuts[-1])
+    for at, begin in enumerate(range(start, columns, chunk)):
+        cuts.insert(2 + 3 * at, (begin, chunk, None, 0))
+
+    stores = []
+    for j, (begin, width, ref, place) in enumerate(cuts):
+        cut = slice(begin, begin + width)
         coeff = messages(cut)
-        if j < len(pieces):
-            ref, place = pieces[j]
-            obuf[:, cut] = ref[:, place : place + chunk] - mm(effect, coeff)
+        if ref is not None:
+            obuf[:, cut] = ref[:, place : place + width] - mm(effect, coeff)
         else:
             for rows, inner in local_part(cut, high_ref, low_ref, sums_ref, cols_ref, solve):
                 obuf[rows, cut] = inner - mm(effect[rows], coeff)
-        cut = pl.ds(j * chunk, chunk)
+        cut = pl.ds(begin, width)
         stores.append(pltpu.make_async_copy(obuf.at[:, cut], out_ref.at[:, cut], sems.at[j]))
         stores[-1].start()
     for store in stores:
@@ -505,7 +517,7 @@
         out_specs=hbm,
         scratch_shapes=[
             pltpu.VMEM((rows, columns), F32),
-            pltpu.SemaphoreType.DMA((chunks,)),
+            pltpu.SemaphoreType.DMA((chunks + 2,)),
         ],
         compiler_params=params,
         cost_estimate=cost(2, rows * columns * 200),

time: 15.5 us -> 15.6 us (level)
  no operation moved by 1% of the time
where the time goes in v4:
time: 15.6 us; the launch traced here: 15.4 us
  Pallas kernels  9.11 us (58%)
  starting transfers between devices  6.08 us (39%)
  waiting for transfers between devices  0.17 us (1%)
    ppermute x1, starting transfers between devices, local(): vectors = (reflectors, lax.ppermute(reflectors, 'col', [(0, 1), (1, 0)]))  2.97 us
    pallas_call x1, Pallas kernels, local(): pl.pallas_call(functools.partial(finish_kernel, chunk), out_shape=shape((...  2.47 us
    pallas_call x1, Pallas kernels, local(): pl.pallas_call(prepare_kernel, out_shape=(shape((rows, columns), BF16), s...  2.32 us
    ppermute x1, starting transfers between devices, local(): got_across = lax.ppermute(across, ('row', 'col'), over_chips)  1.67 us
    pallas_call x1, Pallas kernels, local(): pl.pallas_call(functools.partial(inside_kernel, chunk, len(vectors)), out...  1.39 us
    ppermute x1, starting transfers between devices, local(): got_late = lax.ppermute(late, ('row', 'col'), over_chips)  1.24 us
    pallas_call x1, Pallas kernels, local(): pl.pallas_call(functools.partial(project_kernel, chunk, len(vectors)), ou...  1.22 us
    pallas_call x1, Pallas kernels, local(): pl.pallas_call(functools.partial(inside_more_kernel, chunk, inside_first)...  1.09 us
  transfers between devices with their start and end apart: 5, of which 2 were waited for; matrix products, arithmetic and copies ran while one was open for 0% of the time, Pallas kernels for 35%

profile of v4, /device:TPU:0, one launch (start us, length us, event | category | flops | bytes accessed | tf_op | source)
XLA Modules:
  0.0 15.4 jit_solution(16249120878063430015)
XLA Ops:
  0.0 0.0 copy-start
  0.0 3.0 %collective-permute-start = (f32[8,512]{1,0:T(8,128)}, f32[8,512]{1,0:T(8,128)S(1)}, u32[]{:S(2)}, u32[]{:S(2)}) collective-permute-start(f32[8,512]{1,0:T(8,128)} %refs_0_.3), channel_id=1, source_target_pairs={{0,1},{1,0},{2,3},{3,2},{4,5},{5,4},{6,7},{7,6},{8,9},{9,8},{10,11... | collective-permute-start | bytes 49160 | tf_op jit(solution)/shard_map/ppermute | solution.py:410
  3.0 2.3 %prepare.1 = (bf16[512,2048]{1,0:T(8,128)(2,1)S(1)}, bf16[512,2048]{1,0:T(8,128)(2,1)S(1)}, s32[16,512]{1,0:T(8,128)S(1)}) custom-call(f32[512,2048]{1,0:T(8,128)} %x_ref.1, s32[16]{0:T(128)} %off_ref.1), custom_call_target="tpu_custom_call" | custom-call | bytes 8388608 | tf_op jit(solution)/shard_map/prepare/pallas_call | solution.py:416
  5.3 0.0 collective-permute-done.refs_1_
  5.3 0.0 copy-done
  5.3 1.2 %project.1 = (f32[112,2048]{1,0:T(8,128)S(1)}, f32[8,2176]{1,0:T(8,128)S(1)}, f32[8,2176]{1,0:T(8,128)S(1)}, f32[16,2176]{1,0:T(8,128)S(1)}, f32[16,2176]{1,0:T(8,128)S(1)}, /*index=5*/f32[112,128]{1,0:T(8,128)S(1)}) custom-call(f32[8,512]{1,0:T(8,128)S(1)} %copy-done, f32[8,512]{1,0:T(8,128)S(1)} %collective-permute-done.refs_1_, ...), custom_call_target="tpu_custom_call" | custom-call | flops 251658240 | bytes 8388608 | tf_op jit(solution)/shard_map/project/pallas_call | solution.py:438
  6.5 0.1 collective-permute-start.2
  6.6 1.7 %collective-permute-start.1 = (f32[8,2176]{1,0:T(8,128)S(1)}, f32[8,2176]{1,0:T(8,128)S(1)}, u32[]{:S(2)}, u32[]{:S(2)}) collective-permute-start(f32[8,2176]{1,0:T(8,128)S(1)} %get-tuple-element.22), channel_id=1, source_target_pairs={{2,4},{3,5},{6,8},{7,9},{10,12},{11,13},{14,16},{15,17},{18,20},{1... | collective-permute-start | bytes 208904 | tf_op jit(solution)/shard_map/ppermute | solution.py:470
  8.3 0.0 collective-permute-done.2.got_ref.refs_6_.refs_2_
  8.3 0.3 %complete_even.1.refs_7_ = f32[8,2176]{1,0:T(8,128)S(1)} custom-call(f32[16,2176]{1,0:T(8,128)S(1)} %get-tuple-element.23.down_ref.refs_7_.refs_4_, f32[16,2176]{1,0:T(8,128)S(1)} %get-tuple-element.24.up_ref.refs_8_.refs_5_, f32[8,2176]{1,0:T(8,128)S(1)} %collective-permute-done.2.got_ref.refs_6_.refs_2_), custom_call_target="tpu_custom_call" | custom-call | tf_op jit(solution)/shard_map/complete_even/pallas_call | solution.py:471
  8.6 1.2 %collective-permute-start.3 = (f32[8,2176]{1,0:T(8,128)S(1)}, f32[8,2176]{1,0:T(8,128)S(1)}, u32[]{:S(2)}, u32[]{:S(2)}) collective-permute-start(f32[8,2176]{1,0:T(8,128)S(1)} %complete_even.1.refs_7_), channel_id=1, source_target_pairs={{2,4},{3,5},{6,8},{7,9},{10,12},{11,13},{14,16},{15,17},{18,20},{1... | collective-permute-start | bytes 208904 | tf_op jit(solution)/shard_map/ppermute | solution.py:479
  9.8 1.4 %inside.1 = (f32[512,1024]{1,0:T(8,128)S(1)}, bf16[512,128]{1,0:T(8,128)(2,1)S(1)}, bf16[512,240]{1,0:T(8,128)(2,1)S(1)}) custom-call(f32[8,512]{1,0:T(8,128)S(1)} %copy-done, f32[8,512]{1,0:T(8,128)S(1)} %collective-permute-done.refs_1_, s32[16,512]{1,0:T(8,128)S(1)} %get-tuple-element.19.refs_2_, ...), custom_call_target="tpu_custom_call" | custom-call | flops 251658240 | bytes 8388608 | tf_op jit(solution)/shard_map/inside/pallas_call | solution.py:483
  11.2 0.0 collective-permute-done.1.got_ref.refs_5_.refs_0_
  11.2 0.3 %complete_odd.1 = f32[8,2048]{1,0:T(8,128)S(1)} custom-call(f32[16,2176]{1,0:T(8,128)S(1)} %get-tuple-element.23.down_ref.refs_7_.refs_4_, f32[16,2176]{1,0:T(8,128)S(1)} %get-tuple-element.24.up_ref.refs_8_.refs_5_, f32[8,2176]{1,0:T(8,128)S(1)} %collective-permute-done.1.got_ref.refs_5_.refs_0_, bf16[512,128]{1,0:T(8,128)(2,1)S(1)} %get-tuple-element.28.refs_0_.refs_9_), custom_call_target="tpu_custom_call" | custom-call | tf_op jit(solution)/shard_map/complete_odd/pallas_call | solution.py:493
  11.6 0.1 collective-permute-start.4
  11.7 1.1 %inside_more.1 = (f32[512,512]{1,0:T(8,128)S(1)}, bf16[512,128]{1,0:T(8,128)(2,1)S(1)}) custom-call(bf16[512,2048]{1,0:T(8,128)(2,1)S(1)} %get-tuple-element.20.refs_3_.refs_0_.refs_7_, bf16[512,2048]{1,0:T(8,128)(2,1)S(1)} %get-tuple-element.21.refs_4_.refs_1_.refs_8_, f32[112,2048]{1,0:T(8,128)S(1)} %get-tuple-element.26.refs_5_.refs_2_.refs_9_, ...), custom_call_target="tpu_custom_call" | custom-call | flops 251658240 | bytes 8388608 | tf_op jit(solution)/shard_map/inside_more/pallas_call | solution.py:503
  12.8 0.1 collective-permute-done.4.refs_3_
  12.9 0.1 collective-permute-done.3.refs_1_
  13.0 2.5 %finish.1 = f32[512,2048]{1,0:T(8,128)} custom-call(f32[8,2176]{1,0:T(8,128)S(1)} %collective-permute-done.1.got_ref.refs_5_.refs_0_, f32[8,2176]{1,0:T(8,128)S(1)} %collective-permute-done.3.refs_1_, f32[8,2176]{1,0:T(8,128)S(1)} %collective-permute-done.2.got_ref.refs_6_.refs_2_, f32[8,2048]{1,0:T(8,128)S(1)} %collective-permute-done.4.refs_3_, ...), custom_call_target="tpu_custom_call" | custom-call | flops 209715200 | bytes 8388608 | tf_op jit(solution)/shard_map/finish/pallas_call | solution.py:513
Async XLA Ops:
  0.0 5.3 %copy-start = (f32[8,512]{1,0:T(8,128)S(1)}, f32[8,512]{1,0:T(8,128)}, u32[]{:S(2)}) copy-start(f32[8,512]{1,0:T(8,128)} %refs_0_.3) | copy-start | bytes 49156
  0.0 5.3 %collective-permute-start = (f32[8,512]{1,0:T(8,128)}, f32[8,512]{1,0:T(8,128)S(1)}, u32[]{:S(2)}, u32[]{:S(2)}) collective-permute-start(f32[8,512]{1,0:T(8,128)} %refs_0_.3), channel_id=1, source_target_pairs={{0,1},{1,0},{2,3},{3,2},{4,5},{5,4},{6,7},{7,6},{8,9},{9,8},{10,11... | collective-permute-start | bytes 49160 | tf_op jit(solution)/shard_map/ppermute | solution.py:410
  6.5 1.7 %collective-permute-start.2 = (f32[8,2176]{1,0:T(8,128)S(1)}, f32[8,2176]{1,0:T(8,128)S(1)}, u32[]{:S(2)}, u32[]{:S(2)}) collective-permute-start(f32[8,2176]{1,0:T(8,128)S(1)} %get-tuple-element.25), channel_id=1, source_target_pairs={{0,2},{4,6},{8,10},{12,14},{16,18},{20,22},{24,26},{28,30},{2,0},{... | collective-permute-start | bytes 208904 | tf_op jit(solution)/shard_map/ppermute | solution.py:469
  6.6 4.6 %collective-permute-start.1 = (f32[8,2176]{1,0:T(8,128)S(1)}, f32[8,2176]{1,0:T(8,128)S(1)}, u32[]{:S(2)}, u32[]{:S(2)}) collective-permute-start(f32[8,2176]{1,0:T(8,128)S(1)} %get-tuple-element.22), channel_id=1, source_target_pairs={{2,4},{3,5},{6,8},{7,9},{10,12},{11,13},{14,16},{15,17},{18,20},{1... | collective-permute-start | bytes 208904 | tf_op jit(solution)/shard_map/ppermute | solution.py:470
  8.6 4.4 %collective-permute-start.3 = (f32[8,2176]{1,0:T(8,128)S(1)}, f32[8,2176]{1,0:T(8,128)S(1)}, u32[]{:S(2)}, u32[]{:S(2)}) collective-permute-start(f32[8,2176]{1,0:T(8,128)S(1)} %complete_even.1.refs_7_), channel_id=1, source_target_pairs={{2,4},{3,5},{6,8},{7,9},{10,12},{11,13},{14,16},{15,17},{18,20},{1... | collective-permute-start | bytes 208904 | tf_op jit(solution)/shard_map/ppermute | solution.py:479
  11.6 1.3 %collective-permute-start.4 = (f32[8,2048]{1,0:T(8,128)S(1)}, f32[8,2048]{1,0:T(8,128)S(1)}, u32[]{:S(2)}, u32[]{:S(2)}) collective-permute-start(f32[8,2048]{1,0:T(8,128)S(1)} %complete_odd.1), channel_id=1, source_target_pairs={{0,2},{4,6},{8,10},{12,14},{16,18},{20,22},{24,26},{28,30},{2,0},{... | collective-permute-start | bytes 196616 | tf_op jit(solution)/shard_map/ppermute | solution.py:501

commit v5 on v3

--- a/solution.py
+++ b/solution.py
@@ -467,8 +467,8 @@
     )(down, up, got_beside)
     got_late = lax.ppermute(late, ("row", "col"), over_chips)
 
+    inside_first = (chunks + 1) // 2 * chunk
     inside_next = (chunks + 2) // 4 * chunk
-    inside_first = columns - inside_next
     inner, ends, cols = pl.pallas_call(
         functools.partial(inside_kernel, wide, len(vectors)),
         out_shape=(shape((rows, inside_first), F32), shape((rows, 128), BF16), shape((rows, 3 * BAND), BF16)),
@@ -500,7 +500,7 @@
     )(high, low, sums, solve, cols, got_across, got_beside, down, up, ends)
 
     return pl.pallas_call(
-        functools.partial(finish_kernel, chunk),
+        functools.partial(finish_kernel, wide),
         out_shape=shape((rows, columns), F32),
         in_specs=[vmem] * 14,
         out_specs=hbm,

time: 15.5 us -> 15.5 us (level)
  Pallas kernels: 8.82 us -> 8.47 us
  waiting for transfers between devices: 0.34 us -> 0.68 us
    pallas_call x1, Pallas kernels: 1.39 us -> 1.05 us  [local(): pl.pallas_call(functools.partial(inside_kernel, wide, len(vectors)), out_...]
    ppermute x1, waiting for transfers between devices: 0.08 us -> 0.35 us  [local(): got_late = lax.ppermute(late, ('row', 'col'), over_chips)]
  transfers between devices with their start and end apart: 5 -> 5, of which waited for: 2 -> 3; matrix products, arithmetic and copies ran while one was open for 0% -> 0% of each run, Pallas kernels for 34% -> 32%
where the time goes in v5:
time: 15.5 us; the launch traced here: 15.3 us
  Pallas kernels  8.47 us (55%)
  starting transfers between devices  6.12 us (39%)
  waiting for transfers between devices  0.68 us (4%)
    ppermute x1, starting transfers between devices, local(): vectors = (reflectors, lax.ppermute(reflectors, 'col', [(0, 1), (1, 0)]))  2.97 us
    pallas_call x1, Pallas kernels, local(): pl.pallas_call(functools.partial(finish_kernel, wide), out_shape=shape((r...  2.37 us
    pallas_call x1, Pallas kernels, local(): pl.pallas_call(prepare_kernel, out_shape=(shape((rows, columns), BF16), s...  2.32 us
    ppermute x1, starting transfers between devices, local(): got_across = lax.ppermute(across, ('row', 'col'), over_chips)  1.67 us
    ppermute x1, starting transfers between devices, local(): got_late = lax.ppermute(late, ('row', 'col'), over_chips)  1.24 us
    pallas_call x1, Pallas kernels, local(): pl.pallas_call(functools.partial(project_kernel, wide, len(vectors)), out...  1.22 us
    pallas_call x1, Pallas kernels, local(): pl.pallas_call(functools.partial(inside_kernel, wide, len(vectors)), out_...  1.05 us
    pallas_call x1, Pallas kernels, local(): pl.pallas_call(functools.partial(inside_more_kernel, wide, inside_first),...  0.89 us
  transfers between devices with their start and end apart: 5, of which 3 were waited for; matrix products, arithmetic and copies ran while one was open for 0% of the time, Pallas kernels for 32%

profile of v5, /device:TPU:0, one launch (start us, length us, event | category | flops | bytes accessed | tf_op | source)
XLA Modules:
  0.0 15.3 jit_solution(3782597925904297758)
XLA Ops:
  0.0 0.0 copy-start
  0.0 3.0 %collective-permute-start = (f32[8,512]{1,0:T(8,128)}, f32[8,512]{1,0:T(8,128)S(1)}, u32[]{:S(2)}, u32[]{:S(2)}) collective-permute-start(f32[8,512]{1,0:T(8,128)} %refs_0_.3), channel_id=1, source_target_pairs={{0,1},{1,0},{2,3},{3,2},{4,5},{5,4},{6,7},{7,6},{8,9},{9,8},{10,11... | collective-permute-start | bytes 49160 | tf_op jit(solution)/shard_map/ppermute | solution.py:399
  3.0 2.3 %prepare.1 = (bf16[512,2048]{1,0:T(8,128)(2,1)S(1)}, bf16[512,2048]{1,0:T(8,128)(2,1)S(1)}, s32[16,512]{1,0:T(8,128)S(1)}) custom-call(f32[512,2048]{1,0:T(8,128)} %x_ref.1, s32[16]{0:T(128)} %off_ref.1), custom_call_target="tpu_custom_call" | custom-call | bytes 8388608 | tf_op jit(solution)/shard_map/prepare/pallas_call | solution.py:405
  5.3 0.0 collective-permute-done.refs_1_
  5.3 0.0 copy-done
  5.3 1.2 %project.1 = (f32[112,2048]{1,0:T(8,128)S(1)}, f32[8,2176]{1,0:T(8,128)S(1)}, f32[8,2176]{1,0:T(8,128)S(1)}, f32[16,2176]{1,0:T(8,128)S(1)}, f32[16,2176]{1,0:T(8,128)S(1)}, /*index=5*/f32[112,128]{1,0:T(8,128)S(1)}) custom-call(f32[8,512]{1,0:T(8,128)S(1)} %copy-done, f32[8,512]{1,0:T(8,128)S(1)} %collective-permute-done.refs_1_, ...), custom_call_target="tpu_custom_call" | custom-call | flops 251658240 | bytes 8388608 | tf_op jit(solution)/shard_map/project/pallas_call | solution.py:427
  6.5 0.1 collective-permute-start.2
  6.6 1.7 %collective-permute-start.1 = (f32[8,2176]{1,0:T(8,128)S(1)}, f32[8,2176]{1,0:T(8,128)S(1)}, u32[]{:S(2)}, u32[]{:S(2)}) collective-permute-start(f32[8,2176]{1,0:T(8,128)S(1)} %get-tuple-element.22), channel_id=1, source_target_pairs={{2,4},{3,5},{6,8},{7,9},{10,12},{11,13},{14,16},{15,17},{18,20},{1... | collective-permute-start | bytes 208904 | tf_op jit(solution)/shard_map/ppermute | solution.py:459
  8.3 0.0 collective-permute-done.2.got_ref.refs_6_.refs_2_
  8.3 0.3 %complete_even.1.refs_7_ = f32[8,2176]{1,0:T(8,128)S(1)} custom-call(f32[16,2176]{1,0:T(8,128)S(1)} %get-tuple-element.23.down_ref.refs_7_.refs_4_, f32[16,2176]{1,0:T(8,128)S(1)} %get-tuple-element.24.up_ref.refs_8_.refs_5_, f32[8,2176]{1,0:T(8,128)S(1)} %collective-permute-done.2.got_ref.refs_6_.refs_2_), custom_call_target="tpu_custom_call" | custom-call | tf_op jit(solution)/shard_map/complete_even/pallas_call | solution.py:460
  8.6 1.2 %collective-permute-start.3 = (f32[8,2176]{1,0:T(8,128)S(1)}, f32[8,2176]{1,0:T(8,128)S(1)}, u32[]{:S(2)}, u32[]{:S(2)}) collective-permute-start(f32[8,2176]{1,0:T(8,128)S(1)} %complete_even.1.refs_7_), channel_id=1, source_target_pairs={{2,4},{3,5},{6,8},{7,9},{10,12},{11,13},{14,16},{15,17},{18,20},{1... | collective-permute-start | bytes 208904 | tf_op jit(solution)/shard_map/ppermute | solution.py:468
  9.8 1.0 %inside.1 = (f32[512,1024]{1,0:T(8,128)S(1)}, bf16[512,128]{1,0:T(8,128)(2,1)S(1)}, bf16[512,240]{1,0:T(8,128)(2,1)S(1)}) custom-call(f32[8,512]{1,0:T(8,128)S(1)} %copy-done, f32[8,512]{1,0:T(8,128)S(1)} %collective-permute-done.refs_1_, s32[16,512]{1,0:T(8,128)S(1)} %get-tuple-element.19.refs_2_, ...), custom_call_target="tpu_custom_call" | custom-call | flops 251658240 | bytes 8388608 | tf_op jit(solution)/shard_map/inside/pallas_call | solution.py:472
  10.9 0.1 collective-permute-done.1.got_ref.refs_5_.refs_0_
  11.0 0.3 %complete_odd.1 = f32[8,2048]{1,0:T(8,128)S(1)} custom-call(f32[16,2176]{1,0:T(8,128)S(1)} %get-tuple-element.23.down_ref.refs_7_.refs_4_, f32[16,2176]{1,0:T(8,128)S(1)} %get-tuple-element.24.up_ref.refs_8_.refs_5_, f32[8,2176]{1,0:T(8,128)S(1)} %collective-permute-done.1.got_ref.refs_5_.refs_0_, bf16[512,128]{1,0:T(8,128)(2,1)S(1)} %get-tuple-element.28.refs_0_.refs_9_), custom_call_target="tpu_custom_call" | custom-call | tf_op jit(solution)/shard_map/complete_odd/pallas_call | solution.py:482
  11.3 0.2 %collective-permute-start.4 = (f32[8,2048]{1,0:T(8,128)S(1)}, f32[8,2048]{1,0:T(8,128)S(1)}, u32[]{:S(2)}, u32[]{:S(2)}) collective-permute-start(f32[8,2048]{1,0:T(8,128)S(1)} %complete_odd.1), channel_id=1, source_target_pairs={{0,2},{4,6},{8,10},{12,14},{16,18},{20,22},{24,26},{28,30},{2,0},{... | collective-permute-start | bytes 196616 | tf_op jit(solution)/shard_map/ppermute | solution.py:490
  11.5 0.9 %inside_more.1 = (f32[512,512]{1,0:T(8,128)S(1)}, bf16[512,128]{1,0:T(8,128)(2,1)S(1)}) custom-call(bf16[512,2048]{1,0:T(8,128)(2,1)S(1)} %get-tuple-element.20.refs_3_.refs_0_.refs_7_, bf16[512,2048]{1,0:T(8,128)(2,1)S(1)} %get-tuple-element.21.refs_4_.refs_1_.refs_8_, f32[112,2048]{1,0:T(8,128)S(1)} %get-tuple-element.26.refs_5_.refs_2_.refs_9_, ...), custom_call_target="tpu_custom_call" | custom-call | flops 251658240 | bytes 8388608 | tf_op jit(solution)/shard_map/inside_more/pallas_call | solution.py:492
  12.4 0.2 %collective-permute-done.4.refs_3_ = f32[8,2048]{1,0:T(8,128)S(1)} collective-permute-done((f32[8,2048]{1,0:T(8,128)S(1)}, f32[8,2048]{1,0:T(8,128)S(1)}, u32[]{:S(2)}, u32[]{:S(2)}) %collective-permute-start.4) | collective-permute-done | bytes 65568 | tf_op jit(solution)/shard_map/ppermute | solution.py:490
  12.6 0.4 %collective-permute-done.3.refs_1_ = f32[8,2176]{1,0:T(8,128)S(1)} collective-permute-done((f32[8,2176]{1,0:T(8,128)S(1)}, f32[8,2176]{1,0:T(8,128)S(1)}, u32[]{:S(2)}, u32[]{:S(2)}) %collective-permute-start.3) | collective-permute-done | bytes 69664 | tf_op jit(solution)/shard_map/ppermute | solution.py:468
  13.0 2.4 %finish.1 = f32[512,2048]{1,0:T(8,128)} custom-call(f32[8,2176]{1,0:T(8,128)S(1)} %collective-permute-done.1.got_ref.refs_5_.refs_0_, f32[8,2176]{1,0:T(8,128)S(1)} %collective-permute-done.3.refs_1_, f32[8,2176]{1,0:T(8,128)S(1)} %collective-permute-done.2.got_ref.refs_6_.refs_2_, f32[8,2048]{1,0:T(8,128)S(1)} %collective-permute-done.4.refs_3_, ...), custom_call_target="tpu_custom_call" | custom-call | flops 209715200 | bytes 8388608 | tf_op jit(solution)/shard_map/finish/pallas_call | solution.py:502
Async XLA Ops:
  0.0 5.3 %copy-start = (f32[8,512]{1,0:T(8,128)S(1)}, f32[8,512]{1,0:T(8,128)}, u32[]{:S(2)}) copy-start(f32[8,512]{1,0:T(8,128)} %refs_0_.3) | copy-start | bytes 49156
  0.0 5.3 %collective-permute-start = (f32[8,512]{1,0:T(8,128)}, f32[8,512]{1,0:T(8,128)S(1)}, u32[]{:S(2)}, u32[]{:S(2)}) collective-permute-start(f32[8,512]{1,0:T(8,128)} %refs_0_.3), channel_id=1, source_target_pairs={{0,1},{1,0},{2,3},{3,2},{4,5},{5,4},{6,7},{7,6},{8,9},{9,8},{10,11... | collective-permute-start | bytes 49160 | tf_op jit(solution)/shard_map/ppermute | solution.py:399
  6.5 1.7 %collective-permute-start.2 = (f32[8,2176]{1,0:T(8,128)S(1)}, f32[8,2176]{1,0:T(8,128)S(1)}, u32[]{:S(2)}, u32[]{:S(2)}) collective-permute-start(f32[8,2176]{1,0:T(8,128)S(1)} %get-tuple-element.25), channel_id=1, source_target_pairs={{0,2},{4,6},{8,10},{12,14},{16,18},{20,22},{24,26},{28,30},{2,0},{... | collective-permute-start | bytes 208904 | tf_op jit(solution)/shard_map/ppermute | solution.py:458
  6.6 4.4 %collective-permute-start.1 = (f32[8,2176]{1,0:T(8,128)S(1)}, f32[8,2176]{1,0:T(8,128)S(1)}, u32[]{:S(2)}, u32[]{:S(2)}) collective-permute-start(f32[8,2176]{1,0:T(8,128)S(1)} %get-tuple-element.22), channel_id=1, source_target_pairs={{2,4},{3,5},{6,8},{7,9},{10,12},{11,13},{14,16},{15,17},{18,20},{1... | collective-permute-start | bytes 208904 | tf_op jit(solution)/shard_map/ppermute | solution.py:459
  8.6 4.4 %collective-permute-start.3 = (f32[8,2176]{1,0:T(8,128)S(1)}, f32[8,2176]{1,0:T(8,128)S(1)}, u32[]{:S(2)}, u32[]{:S(2)}) collective-permute-start(f32[8,2176]{1,0:T(8,128)S(1)} %complete_even.1.refs_7_), channel_id=1, source_target_pairs={{2,4},{3,5},{6,8},{7,9},{10,12},{11,13},{14,16},{15,17},{18,20},{1... | collective-permute-start | bytes 208904 | tf_op jit(solution)/shard_map/ppermute | solution.py:468
  11.3 1.3 %collective-permute-start.4 = (f32[8,2048]{1,0:T(8,128)S(1)}, f32[8,2048]{1,0:T(8,128)S(1)}, u32[]{:S(2)}, u32[]{:S(2)}) collective-permute-start(f32[8,2048]{1,0:T(8,128)S(1)} %complete_odd.1), channel_id=1, source_target_pairs={{0,2},{4,6},{8,10},{12,14},{16,18},{20,22},{24,26},{28,30},{2,0},{... | collective-permute-start | bytes 196616 | tf_op jit(solution)/shard_map/ppermute | solution.py:490
